TPU v7x, 32 devices: a whole 2x2x4 slice. The times are simulated.
32 devices in a mesh: seq: 8 (over z, x), dp: 4 (over y, core).
Axes of the slice: x: 2, y: 2, z: 4, core: 2. Of those that a mesh axis runs over, the one named last changes fastest.
Arguments:
- activations: bfloat16 [4, 2048, 8192], P('dp', 'seq'), may hold values from -16 to 16
- query_states: bfloat16 [4, 2048, 4096], P('dp', 'seq'), may hold values from -400 to 400
- key_states: bfloat16 [4, 2048, 512], P('dp', 'seq'), may hold values from -6 to 6
- value_states: bfloat16 [4, 2048, 512], P('dp', 'seq'), may hold values from -6 to 6
- output_grad: bfloat16 [4, 2048, 4096], P('dp', 'seq'), may hold values from -6.5 to 6.5
- query_lowrank: bfloat16 [4, 2048, 16], P('dp', 'seq'), may hold values from -6 to 6
- value_lowrank: bfloat16 [4, 2048, 16], P('dp', 'seq'), may hold values from -6 to 6
- query_up_matrix: bfloat16 [16, 4096], replicated, may hold values from -0.09375 to 0.09375
- value_up_matrix: bfloat16 [16, 512], replicated, may hold values from -0.25 to 0.25
- noise_query_down: float32 [8192, 16], P('seq'), may hold values from -6 to 6
- noise_query_lift: float32 [16, 4096], P(None, 'seq'), may hold values from -6 to 6
- noise_value_down: float32 [8192, 16], P('seq'), may hold values from -6 to 6
- noise_value_lift: float32 [16, 512], P(None, 'seq'), may hold values from -6 to 6
- block_order: int32 [4, 8], P('dp', 'seq'), may hold values from 0 to 7, as said below
- valid_lengths: int32 [4], P('dp'), may hold values from 512 to 2048, as said below
Outputs:
- example_norms: float32 [4], P('dp')
- query_down_sum: float32 [8192, 16], P('seq')
- query_lift_sum: float32 [16, 4096], P(None, 'seq')
- value_down_sum: float32 [8192, 16], P('seq')
- value_lift_sum: float32 [16, 512], P(None, 'seq')
Inputs may be any that keep to these rules, and one draw needn't show every extreme that they name: `valid_lengths`: some example has all 2048 tokens valid in every draw. Each example's stored blocks hold the sequence blocks in cyclic order: block_order[b, j] = (s_b + j) mod 8, with a starting block s_b from 1 to 7.
All inputs are finite; a program needn't handle non-finite values.
Results may differ from a plain program's by a relative error of at most 0.0073.
Values may be sent and summed in bfloat16 or wider, within the bound.
A program may use at most 64 MiB of HBM per device.

v0:
```python
import math

import jax
import jax.numpy as jnp
from jax import lax
from jax.sharding import PartitionSpec as P

HEAD_SIZE = 128
PCOUNT = 335872


ADAPTER_SCALE = 2.0
NOISE_STD = 0.5
STABLE = 0.01
ROPE_BASE = 500000.0


def from_behind(array, axis, by):
    devices = lax.axis_size(axis)
    return lax.ppermute(array, axis, [(i, (i + by) % devices) for i in range(devices)])


def rotate(values, positions, sign):
    row_count = values.shape[0]
    half = HEAD_SIZE // 2
    grid = values.reshape(row_count, -1, HEAD_SIZE)
    freqs = ROPE_BASE ** (-2.0 * jnp.arange(half).astype(jnp.float32) / HEAD_SIZE)
    angle = positions.astype(jnp.float32)[:, None] * freqs[None, :]
    cosine = jnp.cos(angle)[:, None, :]
    sine = sign * jnp.sin(angle)[:, None, :]
    first = grid[..., :half]
    second = grid[..., half:]
    turned = jnp.concatenate([first * cosine - second * sine, first * sine + second * cosine], -1)
    return turned.reshape(row_count, -1)


def window_grads(query_rot, key_rot, value_rows, grad_eff, allowed):
    row_count = query_rot.shape[0]
    key_count = key_rot.shape[0]
    heads_kv = key_rot.shape[1] // HEAD_SIZE
    group = query_rot.shape[1] // key_rot.shape[1]
    scaling = 1.0 / math.sqrt(HEAD_SIZE)
    query_split = jnp.moveaxis(query_rot.reshape(row_count, heads_kv, group, HEAD_SIZE), 1, 0)
    grad_split = jnp.moveaxis(grad_eff.reshape(row_count, heads_kv, group, HEAD_SIZE), 1, 0)
    key_split = jnp.moveaxis(key_rot.reshape(key_count, heads_kv, HEAD_SIZE), 1, 0)
    value_split = jnp.moveaxis(value_rows.reshape(key_count, heads_kv, HEAD_SIZE), 1, 0)

    def one_head(items):
        query_head, grad_head, key_head, value_head = items
        scores = (
            jnp.einsum("tgd,kd->gtk", query_head, key_head, preferred_element_type=jnp.float32)
            * scaling
        )
        scores = jnp.where(allowed[None], scores, -jnp.inf)
        row_max = jnp.max(scores, -1, keepdims=True)
        shifted = jnp.exp(scores - row_max)
        probs = shifted / jnp.sum(shifted, -1, keepdims=True)
        probs_low = probs.astype(jnp.bfloat16)
        attended = jnp.einsum(
            "gtk,kd->tgd", probs_low, value_head, preferred_element_type=jnp.float32
        )
        delta = jnp.sum(grad_head.astype(jnp.float32) * attended, -1)
        dprob = jnp.einsum("tgd,kd->gtk", grad_head, value_head, preferred_element_type=jnp.float32)
        dscore = (probs * (dprob - jnp.transpose(delta)[:, :, None])).astype(jnp.bfloat16)
        query_gradient = (
            jnp.einsum("gtk,kd->tgd", dscore, key_head, preferred_element_type=jnp.float32)
            * scaling
        )
        dvalue = jnp.einsum("gtk,tgd->kd", probs_low, grad_head, preferred_element_type=jnp.float32)
        return (query_gradient, dvalue)

    query_gradient, dvalue = lax.map(one_head, (query_split, grad_split, key_split, value_split))
    query_gradient = jnp.moveaxis(query_gradient, 0, 1).reshape(row_count, -1)
    dvalue = jnp.moveaxis(dvalue, 0, 1).reshape(key_count, -1)
    return (query_gradient, dvalue)


def squares_of(parts):
    return sum((jnp.sum(part * part) for part in parts))


def body(
    activations,
    query_states,
    key_states,
    value_states,
    output_grad,
    query_lowrank,
    value_lowrank,
    query_up_matrix,
    value_up_matrix,
    noise_query_down,
    noise_query_lift,
    noise_value_down,
    noise_value_lift,
    block_order,
    valid_lengths,
):
    row_count = query_states.shape[1]
    offsets = jnp.arange(row_count, dtype=jnp.int32)
    positions = block_order[0, 0] * row_count + offsets
    query_rot = rotate(query_states[0].astype(jnp.float32), positions, 1.0).astype(jnp.bfloat16)
    key_rot = rotate(key_states[0].astype(jnp.float32), positions, 1.0).astype(jnp.bfloat16)
    keep = positions < valid_lengths[0]
    grad_eff = jnp.where(keep[:, None], output_grad[0], jnp.zeros_like(output_grad[0]))
    key_before, value_before, order_before = from_behind(
        (key_rot, value_states[0], block_order[0]), "seq", 1
    )
    key_pos = jnp.concatenate([positions, order_before[0] * row_count + offsets], 0)
    allowed = key_pos[None, :] <= positions[:, None]
    key_window = jnp.concatenate([key_rot, key_before], 0)
    value_window = jnp.concatenate([value_states[0], value_before], 0)
    dquery_rot, dvalue_window = window_grads(query_rot, key_window, value_window, grad_eff, allowed)
    returned = from_behind(dvalue_window[row_count:], "seq", -1)
    value_projected_gradient = (dvalue_window[:row_count] + returned).astype(jnp.bfloat16)
    query_gradient = rotate(dquery_rot, positions, -1.0).astype(jnp.bfloat16)
    acts = activations[0]
    query_upward_gradient = ADAPTER_SCALE * jnp.dot(
        query_lowrank[0].T, query_gradient, preferred_element_type=jnp.float32
    )
    query_reduced_gradient = (
        ADAPTER_SCALE
        * jnp.dot(query_gradient, query_up_matrix.T, preferred_element_type=jnp.float32)
    ).astype(jnp.bfloat16)
    grad_query_down = jnp.dot(acts.T, query_reduced_gradient, preferred_element_type=jnp.float32)
    value_upward_gradient = ADAPTER_SCALE * jnp.dot(
        value_lowrank[0].T, value_projected_gradient, preferred_element_type=jnp.float32
    )
    value_reduced_gradient = (
        ADAPTER_SCALE
        * jnp.dot(value_projected_gradient, value_up_matrix.T, preferred_element_type=jnp.float32)
    ).astype(jnp.bfloat16)
    grad_value_down = jnp.dot(acts.T, value_reduced_gradient, preferred_element_type=jnp.float32)
    whole_qd, whole_ql, whole_vd, whole_vl = lax.psum(
        (grad_query_down, query_upward_gradient, grad_value_down, value_upward_gradient), "seq"
    )
    squares = squares_of((whole_qd, whole_ql, whole_vd, whole_vl))
    place = lax.axis_index("seq")
    count = lax.axis_size("seq")
    down_rows = whole_qd.shape[0] // count
    query_cols = whole_ql.shape[1] // count
    value_cols = whole_vl.shape[1] // count
    share_qd = lax.dynamic_slice_in_dim(whole_qd, place * down_rows, down_rows, 0)
    share_ql = lax.dynamic_slice_in_dim(whole_ql, place * query_cols, query_cols, 1)
    share_vd = lax.dynamic_slice_in_dim(whole_vd, place * down_rows, down_rows, 0)
    share_vl = lax.dynamic_slice_in_dim(whole_vl, place * value_cols, value_cols, 1)
    norm_value = jnp.sqrt(squares)
    factor = math.sqrt(PCOUNT) / (norm_value + STABLE)
    summed_qd, summed_ql, summed_vd, summed_vl = lax.psum(
        (factor * share_qd, factor * share_ql, factor * share_vd, factor * share_vl), "dp"
    )
    example_norms = norm_value.reshape(1)
    return (
        example_norms,
        summed_qd + NOISE_STD * noise_query_down,
        summed_ql + NOISE_STD * noise_query_lift,
        summed_vd + NOISE_STD * noise_value_down,
        summed_vl + NOISE_STD * noise_value_lift,
    )


def solution(mesh):
    in_specs = (
        P("dp", "seq", None),
        P("dp", "seq", None),
        P("dp", "seq", None),
        P("dp", "seq", None),
        P("dp", "seq", None),
        P("dp", "seq", None),
        P("dp", "seq", None),
        P(),
        P(),
        P("seq", None),
        P(None, "seq"),
        P("seq", None),
        P(None, "seq"),
        P("dp", "seq"),
        P("dp"),
    )
    out_specs = (P("dp"), P("seq", None), P(None, "seq"), P("seq", None), P(None, "seq"))
    return jax.shard_map(body, mesh=mesh, in_specs=in_specs, out_specs=out_specs, check_vma=False)
```

profile of v0, /device:TPU:0, one launch (start us, length us, event | category | flops | bytes accessed | tf_op | source)
XLA Modules:
  0.0 259.5 jit_solution(11357507719290772713)
XLA Ops:
  7.2 3.0 %collective-permute-start.1 = (s32[1]{0:T(128)}, s32[1]{0:T(128)}, u32[]{:S(2)}, u32[]{:S(2)}) collective-permute-start(s32[1]{0:T(128)} %bitcast.13), channel_id=1, source_target_pairs={{0,4},{4,8},{8,12},{12,16},{16,20},{20,24},{24,28},{28,0},{1,5},{5... | collective-permute-start | bytes 20 | tf_op jit(solution)/shard_map/ppermute | solution.py:20
  11.3 1.6 collective-permute-start.2
  15.1 1.5 collective-permute-start
  17.3 4.2 %copy.36 = bf16[1,256,4096]{1,2,0:T(8,128)(2,1)} copy(bf16[1,256,4096]{2,1,0:T(8,128)(2,1)} %param.21) | data formatting | bytes 4194304 | tf_op args[4]
  21.6 2.9 %copy.45 = f32[1,256,4096]{1,2,0:T(8,128)} copy(bf16[1,256,4096]{2,1,0:T(8,128)(2,1)S(1)} %copy-done.4) | data formatting | bytes 6291456 | tf_op jit(solution)/shard_map/convert_element_type | solution.py:102
  24.5 3.1 %subtract_convert_fusion = (bf16[256,32,64]{0,2,1:T(8,128)(2,1)S(1)}, bf16[256,32,64]{0,2,1:T(8,128)(2,1)S(1)}) fusion(f32[256,32,128]{0,2,1:T(8,128)} %bitcast.169, f32[256,64]{0,1:T(8,128)S(1)} %get-tuple-element.117, f32[256,64]{0,1:T(8,128)S(1)} %get-tuple-element.118), kind=kLoop, calls=%fused_computation.54 | loop fusion | flops 4194304 | bytes 6422528 | tf_op jit(solution)/shard_map/convert.4
  27.7 1.5 pad_maximum_fusion
  29.3 4.0 %copy.33 = bf16[256,32,128]{2,0,1:T(8,128)(2,1)} copy(bf16[256,32,128]{0,2,1:T(8,128)(2,1)} %pad_maximum_fusion) | data formatting | bytes 4194304 | tf_op jit(solution)/shard_map/concatenate | solution.py:33
  35.7 52.4 %while.13 = (s32[]{:T(128)}, f32[4,256,8,128]{1,3,2,0:T(8,128)}, f32[4,512,128]{1,2,0:T(8,128)}, bf16[4,512,128]{1,2,0:T(8,128)(2,1)}, bf16[4,256,8,128]{3,1,2,0...) while((s32[]{:T(128)}, f32[4,256,8,128]{1,3,2,0:T(8,128)}, ...), condition=%wide.region_4.5_spmd.clone, body=%wide.region_0.4_spmd.clone.sunk | while | flops 1355938304 | bytes 52477100 | solution.py:72
  36.1 1.9 fusion.88
  38.0 1.8 fusion.89
  40.2 1.6 copy-done.1
  41.8 1.1 fusion.91
  42.9 1.5 fusion.93
  44.5 4.3 %fusion.92 = f32[4,256,8,128]{1,3,2,0:T(8,128)} fusion(f32[4,256,8,128]{1,3,2,0:T(8,128)} %get-tuple-element.191, s32[]{:T(128)S(6)} %copy.62, f32[8,256]{1,0:T(8,128)S(1)} %bitcast.181, f32[8,256,512]{1,2,0:T(8,128)} %copy-done.1, f32[8,256]{1,0:T(8,128)S(1)} %get-tuple-element.179, bf16[4,512,128]{1,2,0:T(8,128)(2,1)} %get-tuple-element.203, ...), kind=kOutput, calls=%fused_computation.18.clone.1 | convolution fusion | flops 541327360 | bytes 6047744 | tf_op jit(solution)/shard_map/while/body/eval_jaxpr/gtk,kd->tgd/dot_general | solution.py:66
  49.2 1.9 fusion.88
  51.1 1.8 fusion.89
  53.3 1.6 copy-done.1
  56.0 1.5 fusion.93
  57.6 4.3 %fusion.92 = f32[4,256,8,128]{1,3,2,0:T(8,128)} fusion(f32[4,256,8,128]{1,3,2,0:T(8,128)} %get-tuple-element.191, s32[]{:T(128)S(6)} %copy.62, f32[8,256]{1,0:T(8,128)S(1)} %bitcast.181, f32[8,256,512]{1,2,0:T(8,128)} %copy-done.1, f32[8,256]{1,0:T(8,128)S(1)} %get-tuple-element.179, bf16[4,512,128]{1,2,0:T(8,128)(2,1)} %get-tuple-element.203, ...), kind=kOutput, calls=%fused_computation.18.clone.1 | convolution fusion | flops 541327360 | bytes 6047744 | tf_op jit(solution)/shard_map/while/body/eval_jaxpr/gtk,kd->tgd/dot_general | solution.py:66
  62.4 1.9 fusion.88
  64.2 1.8 fusion.89
  66.5 1.6 copy-done.1
  69.2 1.5 fusion.93
  70.7 4.3 %fusion.92 = f32[4,256,8,128]{1,3,2,0:T(8,128)} fusion(f32[4,256,8,128]{1,3,2,0:T(8,128)} %get-tuple-element.191, s32[]{:T(128)S(6)} %copy.62, f32[8,256]{1,0:T(8,128)S(1)} %bitcast.181, f32[8,256,512]{1,2,0:T(8,128)} %copy-done.1, f32[8,256]{1,0:T(8,128)S(1)} %get-tuple-element.179, bf16[4,512,128]{1,2,0:T(8,128)(2,1)} %get-tuple-element.203, ...), kind=kOutput, calls=%fused_computation.18.clone.1 | convolution fusion | flops 541327360 | bytes 6047744 | tf_op jit(solution)/shard_map/while/body/eval_jaxpr/gtk,kd->tgd/dot_general | solution.py:66
  75.5 1.9 fusion.88
  77.3 1.8 fusion.89
  79.6 1.6 copy-done.1
  81.2 1.1 fusion.91
  82.3 1.5 fusion.93
  83.8 4.3 %fusion.92 = f32[4,256,8,128]{1,3,2,0:T(8,128)} fusion(f32[4,256,8,128]{1,3,2,0:T(8,128)} %get-tuple-element.191, s32[]{:T(128)S(6)} %copy.62, f32[8,256]{1,0:T(8,128)S(1)} %bitcast.181, f32[8,256,512]{1,2,0:T(8,128)} %copy-done.1, f32[8,256]{1,0:T(8,128)S(1)} %get-tuple-element.179, bf16[4,512,128]{1,2,0:T(8,128)(2,1)} %get-tuple-element.203, ...), kind=kOutput, calls=%fused_computation.18.clone.1 | convolution fusion | flops 541327360 | bytes 6047744 | tf_op jit(solution)/shard_map/while/body/eval_jaxpr/gtk,kd->tgd/dot_general | solution.py:66
  88.1 2.1 fusion.55
  90.2 3.2 %collective-permute-start.3 = (f32[256,512]{0,1:T(8,128)}, f32[256,512]{0,1:T(8,128)S(1)}, u32[]{:S(2)}, u32[]{:S(2)}) collective-permute-start(f32[256,512]{0,1:T(8,128)} %bitcast.25), channel_id=1, source_target_pairs={{0,28},{4,0},{8,4},{12,8},{16,12},{20,16},{24,20},{28,24},{1,29},{... | collective-permute-start | bytes 1572872 | tf_op jit(solution)/shard_map/ppermute | solution.py:20
  93.4 2.9 %multiply_subtract_fusion = (bf16[256,32,64]{0,2,1:T(8,128)(2,1)S(1)}, bf16[256,32,64]{0,2,1:T(8,128)(2,1)S(1)}) fusion(f32[256,32,128]{0,2,1:T(8,128)} %bitcast.172, f32[256,64]{0,1:T(8,128)S(1)} %get-tuple-element.116, f32[256,64]{0,1:T(8,128)S(1)} %get-tuple-element.118), kind=kLoop, calls=%fused_computation.51 | loop fusion | flops 4194304 | bytes 6422528 | tf_op jit(solution)/shard_map/sub | solution.py:33
  97.0 1.4 fusion.39
  98.4 5.5 %convolution_bitcast_fusion.3 = f32[8192,16]{0,1:T(8,128)} fusion(bf16[1,256,8192]{2,1,0:T(8,128)(2,1)} %param.17, bf16[256,4096]{0,1:T(8,128)(2,1)S(1)} %bitcast.168, bf16[16,4096]{1,0:T(8,128)(2,1)S(1)} %copy-done), kind=kOutput, calls=%fused_computation.43 | convolution fusion | flops 100671488 | bytes 6946816 | tf_op jit(solution)/shard_map/dot_general | solution.py:125
  104.2 4.0 %convolution_bitcast_fusion.2 = f32[8192,16]{0,1:T(8,128)} fusion(bf16[1,256,8192]{2,1,0:T(8,128)(2,1)} %param.17, bf16[256,512]{0,1:T(8,128)(2,1)S(1)} %fusion.45, bf16[16,512]{1,0:T(8,128)(2,1)S(1)} %copy-done.8), kind=kOutput, calls=%fused_computation.42 | convolution fusion | flops 71311360 | bytes 4997120 | tf_op jit(solution)/shard_map/dot_general | solution.py:133
  108.5 38.7 %psum.59 = f32[16,512]{1,0:T(8,128)S(1)} all-reduce(f32[16,512]{1,0:T(8,128)S(1)} %fusion.44), channel_id=1, replica_groups=mesh['seq'=8,'dp'=4] {'seq'}, use_global_device_ids=true, to_apply=%region_11.12 | all-reduce | flops 8192 | bytes 65536 | tf_op jit(solution)/shard_map/psum | solution.py:134
  147.8 46.8 %all-reduce.6.cloned.1.call-done = (f32[8192,16]{0,1:T(8,128)}, f32[16,4096]{1,0:T(8,128)}, f32[8192,16]{0,1:T(8,128)}) async-done(((f32[8192,16]{0,1:T(8,128)}, f32[16,4096]{1,0:T(8,128)}, f32[8192,16]{0,1:T(8,128)}), (f32[8192,16]{0,1:T(8,128)}, f32[16,4096]{1,0:T(8,128)}, f32[8192,16]{0,1:T(8,128)})) %all-reduce.6.cloned.1.call-update) | async-done | bytes 1310736 | tf_op jit(solution)/shard_map/psum | solution.py:134
  194.6 1.8 multiply_reduce_fusion
  196.4 1.6 multiply_reduce_fusion.2
  198.0 1.8 multiply_reduce_fusion.1
  202.4 1.5 dynamic-slice_multiply_fusion
  203.9 1.5 dynamic-slice_multiply_fusion.1
  206.2 11.7 %all-reduce.1 = (f32[16,512]{1,0:T(8,128)S(1)}, f32[16,64]{1,0:T(8,128)S(1)}) all-reduce(f32[16,512]{1,0:T(8,128)S(1)} %dynamic-slice_multiply_fusion.2, f32[16,64]{1,0:T(8,128)S(1)} %dynamic-slice_multiply_fusion.3), channel_id=1, replica_groups=mesh['seq'=8,'dp'=4] {'dp'}, use_global_device_ids=true, to_apply=%region_14.15 | all-reduce | flops 9216 | bytes 73728 | tf_op jit(solution)/shard_map/psum | solution.py:149
  219.2 29.4 %all-reduce.8.cloned.1.call-done = (f32[1024,16]{0,1:T(8,128)}, f32[1024,16]{0,1:T(8,128)}) async-done(((f32[1024,16]{0,1:T(8,128)}, f32[1024,16]{0,1:T(8,128)}), (f32[1024,16]{0,1:T(8,128)}, f32[1024,16]{0,1:T(8,128)})) %all-reduce.8.cloned.1.call-update) | async-done | bytes 131088 | tf_op jit(solution)/shard_map/psum | solution.py:149
  248.6 1.5 multiply_add_fusion.2
  250.1 1.5 multiply_add_fusion.1
  (81 shorter events, 13.9 us)
Async XLA Ops:
  7.2 91.2 %copy-start = (bf16[16,4096]{1,0:T(8,128)(2,1)S(1)}, bf16[16,4096]{1,0:T(8,128)(2,1)}, u32[]{:S(2)}) copy-start(bf16[16,4096]{1,0:T(8,128)(2,1)} %param.24) | copy-start | bytes 393220
  7.2 187.4 %all-reduce.6.cloned.1.call-start = ((), (), s32[]{:S(2)}) async-start(), calls=%async_computation | async-start | bytes 2621440 | tf_op jit(solution)/shard_map/psum | solution.py:134
  7.2 26.1 %collective-permute-start.1 = (s32[1]{0:T(128)}, s32[1]{0:T(128)}, u32[]{:S(2)}, u32[]{:S(2)}) collective-permute-start(s32[1]{0:T(128)} %bitcast.13), channel_id=1, source_target_pairs={{0,4},{4,8},{8,12},{12,16},{16,20},{20,24},{24,28},{28,0},{1,5},{5... | collective-permute-start | bytes 20 | tf_op jit(solution)/shard_map/ppermute | solution.py:20
  11.3 22.7 %collective-permute-start.2 = (bf16[256,512]{0,1:T(8,128)(2,1)S(1)}, bf16[256,512]{0,1:T(8,128)(2,1)S(1)}, u32[]{:S(2)}, u32[]{:S(2)}) collective-permute-start(bf16[256,512]{0,1:T(8,128)(2,1)S(1)} %bitcast.176), channel_id=1, source_target_pairs={{0,4},{4,8},{8,12},{12,16},{16,20},{20,24},{24,28},{28,0},{1,5},{5... | collective-permute-start | bytes 786440 | tf_op jit(solution)/shard_map/ppermute | solution.py:20
  15.1 19.7 %collective-permute-start = (bf16[256,512]{0,1:T(8,128)(2,1)S(1)}, bf16[256,512]{0,1:T(8,128)(2,1)S(1)}, u32[]{:S(2)}, u32[]{:S(2)}) collective-permute-start(bf16[256,512]{0,1:T(8,128)(2,1)S(1)} %bitcast.178), channel_id=1, source_target_pairs={{0,4},{4,8},{8,12},{12,16},{16,20},{20,24},{24,28},{28,0},{1,5},{5... | collective-permute-start | bytes 786440 | tf_op jit(solution)/shard_map/ppermute | solution.py:20
  17.3 4.2 %copy-start.4 = (bf16[1,256,4096]{2,1,0:T(8,128)(2,1)S(1)}, bf16[1,256,4096]{2,1,0:T(8,128)(2,1)}, u32[]{:S(2)}) copy-start(bf16[1,256,4096]{2,1,0:T(8,128)(2,1)} %param.18) | copy-start | bytes 6291460
  24.5 3.1 %copy-start.2 = (bf16[1,256,4096]{1,2,0:T(8,128)(2,1)S(1)}, bf16[1,256,4096]{1,2,0:T(8,128)(2,1)}, u32[]{:S(2)}) copy-start(bf16[1,256,4096]{1,2,0:T(8,128)(2,1)} %copy.36) | copy-start | bytes 6291460
  39.8 2.0 copy-start.1
  39.9 2.0 copy-start.3
  52.9 2.0 copy-start.1
  53.0 2.0 copy-start.3
  66.1 2.0 copy-start.1
  66.1 2.0 copy-start.3
  79.2 2.0 copy-start.1
  79.2 2.0 copy-start.3
  90.2 13.9 %collective-permute-start.3 = (f32[256,512]{0,1:T(8,128)}, f32[256,512]{0,1:T(8,128)S(1)}, u32[]{:S(2)}, u32[]{:S(2)}) collective-permute-start(f32[256,512]{0,1:T(8,128)} %bitcast.25), channel_id=1, source_target_pairs={{0,28},{4,0},{8,4},{12,8},{16,12},{20,16},{24,20},{28,24},{1,29},{... | collective-permute-start | bytes 1572872 | tf_op jit(solution)/shard_map/ppermute | solution.py:20
  96.3 0.7 copy-start.9
  98.4 5.7 %copy-start.8 = (bf16[16,512]{1,0:T(8,128)(2,1)S(1)}, bf16[16,512]{1,0:T(8,128)(2,1)}, u32[]{:S(2)}) copy-start(bf16[16,512]{1,0:T(8,128)(2,1)} %param.25) | copy-start | bytes 49156
  104.2 4.1 %copy-start.10 = (bf16[1,256,16]{1,2,0:T(8,128)(2,1)S(1)}, bf16[1,256,16]{1,2,0:T(8,128)(2,1)}, u32[]{:S(2)}) copy-start(bf16[1,256,16]{1,2,0:T(8,128)(2,1)} %param.23) | copy-start | bytes 24580
  108.2 109.7 %copy-start.7 = (f32[16,512]{1,0:T(8,128)S(1)}, f32[16,512]{1,0:T(8,128)}, u32[]{:S(2)}) copy-start(f32[16,512]{1,0:T(8,128)} %param.27) | copy-start | bytes 98308
  108.2 110.4 %copy-start.11 = (f32[16,64]{1,0:T(8,128)S(1)}, f32[16,64]{1,0:T(8,128)}, u32[]{:S(2)}) copy-start(f32[16,64]{1,0:T(8,128)} %param.29) | copy-start | bytes 12292
  108.2 140.4 %copy-start.5 = (f32[1024,16]{0,1:T(8,128)S(1)}, f32[1024,16]{0,1:T(8,128)}, u32[]{:S(2)}) copy-start(f32[1024,16]{0,1:T(8,128)} %param.26) | copy-start | bytes 196612
  108.2 141.9 %copy-start.6 = (f32[1024,16]{0,1:T(8,128)S(1)}, f32[1024,16]{0,1:T(8,128)}, u32[]{:S(2)}) copy-start(f32[1024,16]{0,1:T(8,128)} %param.28) | copy-start | bytes 196612
  108.2 140.4 %all-reduce.8.cloned.1.call-start = ((), (), s32[]{:S(2)}) async-start(), calls=%async_computation.1 | async-start | bytes 262144 | tf_op jit(solution)/shard_map/psum | solution.py:149
Sparse Core Ops, SparseCore 0:
  108.4 86.1 all-reduce.5
  218.7 29.8 all-reduce.7
where the time goes:
time: 261 us; the launch traced here: 260 us
  waiting for transfers between devices  76.5 us (29%)
  blocking collectives  50.3 us (19%)
  matrix products  46.2 us (18%)
  other arithmetic  33.1 us (13%)
  local copies, waits for them, and re-layouts  23.7 us (9%)
  between operations  20 us (8%)
  starting transfers between devices  9.45 us (4%)
    psum x1, waiting for transfers between devices, body(): lax.psum((grad_query_down, query_upward_gradient, grad_value_down, value_...  46.8 us
    psum x1, blocking collectives, body(): lax.psum((grad_query_down, query_upward_gradient, grad_value_down, value_...  38.7 us
    psum x1, waiting for transfers between devices, body(): lax.psum((factor * share_qd, factor * share_ql, factor * share_vd, factor...  29.4 us
    dot_general x4, matrix products, one_head(): jnp.einsum('gtk,kd->tgd', dscore, key_head, preferred_element_type=jnp.fl...  17.2 us
    psum x1, blocking collectives, body(): lax.psum((factor * share_qd, factor * share_ql, factor * share_vd, factor...  11.7 us
    ppermute x4, starting transfers between devices, from_behind(): lax.ppermute(array, axis, [(i, (i + by) % devices) for i in range(devices)])  9.37 us
    dot_general x4, matrix products, one_head(): jnp.einsum('tgd,kd->gtk', query_head, key_head, preferred_element_type=jn...  7.41 us
    sub x4, other arithmetic, one_head(): shifted = jnp.exp(scores - row_max)  7.39 us
  transfers between devices with their start and end apart: 6, of which 3 were waited for; matrix products, arithmetic and copies ran while one was open for 12% of the time, Pallas kernels for 0%

commit v1 on v0

v1 whole, which is shorter than its diff:
```python
import functools
import math

import jax
import jax.numpy as jnp
from jax import lax
from jax.experimental import pallas as pl
from jax.experimental.pallas import tpu as pltpu
from jax.sharding import PartitionSpec as P

HEAD = 128
PCOUNT = 335872
ADAPTER_SCALE = 2.0
NOISE_STD = 0.5
STABLE = 0.01
ROPE_BASE = 500000.0
NEG = -1e30
F32 = jnp.float32
BF16 = jnp.bfloat16
MESH = pl.DeviceIdType.MESH


def dot(a, b):
    return jnp.dot(a, b, preferred_element_type=F32)


def dot_nt(a, b):
    return lax.dot_general(a, b, (((1,), (1,)), ((), ())), preferred_element_type=F32)


def lane_piece(x, j, width):
    if width >= HEAD:
        return x
    if j:
        x = pltpu.roll(x, HEAD - j * width, 1)
    lanes = lax.broadcasted_iota(jnp.int32, x.shape, 1)
    return jnp.where(lanes < width, x, 0.0)


def kernel(
    n,
    m,
    order_ref,
    valid_ref,
    q_hbm,
    g_hbm,
    acts_hbm,
    k_ref,
    v_ref,
    cos_ref,
    sin_ref,
    qlt_ref,
    vlt_ref,
    qup_ref,
    vup_ref,
    nqd_ref,
    nql_ref,
    nvd_ref,
    nvl_ref,
    norm_ref,
    oqd_ref,
    oql_ref,
    ovd_ref,
    ovl_ref,
    q_scr,
    g_scr,
    acts_scr,
    kwin,
    vwin,
    vlt_prev,
    kt_scr,
    cost_scr,
    sint_scr,
    dv_scr,
    dlq_scr,
    dlv_scr,
    ret_send,
    ret_recv,
    send_d,
    recv_d,
    send_l,
    recv_l,
    acc_d,
    acc_l,
    share_d,
    share_l,
    peer_d,
    peer_l,
    sq_send,
    sq_recv,
    fac_send,
    fac_recv,
    local_sem,
    halo_ssem,
    halo_rsem,
    ret_ssem,
    ret_rsem,
    l_ssem,
    l_rsem,
    dq_ssem,
    dq_rsem,
    dv_ssem,
    dv_rsem,
    sq_ssem,
    sq_rsem,
    shd_ssem,
    shd_rsem,
    shl_ssem,
    shl_rsem,
    fac_ssem,
    fac_rsem,
):
    me = lax.axis_index("seq")
    ex = lax.axis_index("dp")
    right = lax.rem(me + 1, n)
    left = lax.rem(me + n - 1, n)
    tok = k_ref.shape[0]
    groups = k_ref.shape[1] // HEAD
    heads = q_scr.shape[1] // (groups * HEAD)
    wd = acts_scr.shape[1] // n
    wq = q_scr.shape[1] // n
    wqp = max(wq, HEAD)
    wv = k_ref.shape[1] // n
    scaling = 1.0 / math.sqrt(HEAD)
    c2 = scaling * math.log2(math.e)

    load_q = pltpu.make_async_copy(q_hbm, q_scr, local_sem.at[0])
    load_g = pltpu.make_async_copy(g_hbm, g_scr, local_sem.at[1])
    load_acts = pltpu.make_async_copy(acts_hbm, acts_scr, local_sem.at[2])
    load_q.start()
    load_g.start()
    load_acts.start()

    barrier = pltpu.get_barrier_semaphore()

    def greet_seq(k, _):
        peer = lax.rem(me + k, n)
        pl.semaphore_signal(barrier, inc=1, device_id={"seq": peer}, device_id_type=MESH)
        return 0

    lax.fori_loop(1, n, greet_seq, 0)
    for k in range(1, m):
        peer = lax.rem(ex + k, m)
        pl.semaphore_signal(barrier, inc=1, device_id={"dp": peer}, device_id_type=MESH)

    cos = cos_ref[...]
    sin = sin_ref[...]
    for c in range(groups):
        cols = slice(c * HEAD, (c + 1) * HEAD)
        k = k_ref[:, cols].astype(F32)
        kr = k * cos + pltpu.roll(k, HEAD // 2, 1) * sin
        kwin[0:tok, cols] = kr.astype(BF16)
        kt_scr[cols, 0:tok] = kr.T.astype(BF16)
    pl.semaphore_wait(barrier, n - 1 + m - 1)

    def halo(i, src, dst):
        return pltpu.make_async_remote_copy(
            src_ref=src,
            dst_ref=dst,
            send_sem=halo_ssem.at[i],
            recv_sem=halo_rsem.at[i],
            device_id={"seq": right},
            device_id_type=MESH,
        )

    halos = [
        halo(0, kwin.at[pl.ds(0, tok)], kwin.at[pl.ds(tok, tok)]),
        halo(1, v_ref, vwin.at[pl.ds(tok, tok)]),
        halo(2, vlt_ref, vlt_prev),
    ]
    for h in halos:
        h.start()
    vwin[0:tok, :] = v_ref[...]
    cost_scr[...] = cos.T
    sint_scr[...] = sin.T
    send_l[...] = jnp.zeros_like(send_l)
    dlq_scr[...] = jnp.zeros_like(dlq_scr)
    dlv_scr[...] = jnp.zeros_like(dlv_scr)

    order = order_ref[0, 0]
    valid = valid_ref[0]
    rows = lax.broadcasted_iota(jnp.int32, (tok, HEAD), 0) + order * tok
    keep = jnp.where(rows < valid, 1.0, 0.0).astype(BF16)
    bias = jnp.where(order > 0, 0.0, NEG).astype(F32)

    load_q.wait()

    def rope_queries(h, _):
        cols = pl.ds(pl.multiple_of(h * HEAD, HEAD), HEAD)
        q = q_scr[:, cols].astype(F32)
        q_scr[:, cols] = (q * cos_ref[...] + pltpu.roll(q, HEAD // 2, 1) * sin_ref[...]).astype(BF16)
        return 0

    lax.fori_loop(0, groups * heads, rope_queries, 0, unroll=4)
    load_g.wait()
    for h in halos:
        h.wait()
    for c in range(groups):
        cols = slice(c * HEAD, (c + 1) * HEAD)
        kt_scr[cols, tok : 2 * tok] = kwin[tok : 2 * tok, cols].astype(F32).T.astype(BF16)

    key_at = lax.broadcasted_iota(jnp.int32, (tok, tok), 0)
    row_at = lax.broadcasted_iota(jnp.int32, (tok, tok), 1)
    causal = key_at <= row_at

    def one_head(c, i):
        h = c * heads + i
        kcols = pl.ds(pl.multiple_of(c * HEAD, HEAD), HEAD)
        cols = pl.ds(pl.multiple_of(h * HEAD, HEAD), HEAD)
        qr = q_scr[:, cols]
        g = g_scr[:, cols] * keep
        s = dot_nt(kwin[:, kcols], qr)
        own = jnp.where(causal, s[:tok], NEG)
        prev = s[tok:]
        top = jnp.maximum(
            jnp.max(own, 0, keepdims=True), jnp.max(prev, 0, keepdims=True) + bias
        )
        shift = top * c2
        e_own = jnp.exp2(own * c2 - shift)
        e_prev = jnp.exp2(prev * c2 - (shift - bias))
        total = jnp.sum(e_own, 0, keepdims=True) + jnp.sum(e_prev, 0, keepdims=True)
        p = jnp.concatenate([e_own, e_prev], 0) * (1.0 / total)
        dp = dot_nt(vwin[:, kcols], g)
        delta = jnp.sum(p * dp, 0, keepdims=True)
        ds = (p * (dp - delta)).astype(BF16)
        dv = dot(p.astype(BF16), g)
        dq = dot(kt_scr[kcols, :], ds) * scaling
        half = HEAD // 2
        swapped = jnp.concatenate([dq[half:], dq[:half]], 0)
        dq_low = (dq * cost_scr[...] - swapped * sint_scr[...]).astype(BF16)
        lift = ADAPTER_SCALE * dot_nt(qlt_ref[...], dq_low)
        dlq = dot(qup_ref[:, cols], dq_low)
        if wq >= HEAD:
            slot = h * HEAD // wq
            at = pl.multiple_of(lax.rem(h * HEAD, wq), HEAD)
            send_l[slot, :, pl.ds(at, HEAD)] = lift.astype(BF16)
        else:
            per = HEAD // wq
            for j in range(per):
                send_l[h * per + j, :, 0:HEAD] = lane_piece(lift, j, wq).astype(BF16)
        return dv, dlq

    unroll = 4

    def one_group(c, _):
        dv_scr[...] = jnp.zeros_like(dv_scr)

        def some_heads(step, _):
            dvs = None
            dlqs = None
            for u in range(unroll):
                dv, dlq = one_head(c, step * unroll + u)
                dvs = dv if dvs is None else dvs + dv
                dlqs = dlq if dlqs is None else dlqs + dlq
            dv_scr[...] += dvs
            dlq_scr[...] += dlqs
            return 0

        lax.fori_loop(0, heads // unroll, some_heads, 0)
        kcols = pl.ds(pl.multiple_of(c * HEAD, HEAD), HEAD)
        dv_low = dv_scr[...].astype(BF16)
        vup = vup_ref[:, kcols]
        dlv_scr[...] += dot_nt(vup, dv_low)
        vlift = ADAPTER_SCALE * (dot(vlt_ref[...], dv_low[:tok]) + dot(vlt_prev[...], dv_low[tok:]))
        per = HEAD // wv
        for j in range(per):
            send_l[c * per + j, :, wqp : wqp + HEAD] = lane_piece(vlift, j, wv).astype(BF16)
        return 0

    lax.fori_loop(0, groups, one_group, 0)

    ret_send[...] = dlv_scr[:, tok : 2 * tok]
    ret = pltpu.make_async_remote_copy(
        src_ref=ret_send,
        dst_ref=ret_recv,
        send_sem=ret_ssem,
        recv_sem=ret_rsem,
        device_id={"seq": left},
        device_id_type=MESH,
    )
    ret.start()

    def to_seq(src, dst, ssem, rsem, peer, slot):
        return pltpu.make_async_remote_copy(
            src_ref=src,
            dst_ref=dst,
            send_sem=ssem.at[peer],
            recv_sem=rsem.at[slot],
            device_id={"seq": peer},
            device_id_type=MESH,
        )

    def lift_copy(peer, slot):
        return to_seq(send_l.at[peer], recv_l.at[slot], l_ssem, l_rsem, peer, slot)

    half_rows = qlt_ref.shape[0]

    def query_copy(peer, slot):
        return to_seq(
            send_d.at[peer, pl.ds(0, half_rows)],
            recv_d.at[slot, pl.ds(0, half_rows)],
            dq_ssem,
            dq_rsem,
            peer,
            slot,
        )

    def value_copy(peer, slot):
        return to_seq(
            send_d.at[peer, pl.ds(half_rows, half_rows)],
            recv_d.at[slot, pl.ds(half_rows, half_rows)],
            dv_ssem,
            dv_rsem,
            peer,
            slot,
        )

    def send_lift(k, _):
        lift_copy(lax.rem(me + k, n), me).start()
        return 0

    lax.fori_loop(1, n, send_lift, 0)

    load_acts.wait()
    dlow_query = (ADAPTER_SCALE * dlq_scr[...]).astype(BF16)

    def down(low, slot):
        return dot(low, acts_scr[:, pl.ds(pl.multiple_of(slot * wd, wd), wd)])

    def send_query(k, _):
        peer = lax.rem(me + k, n)
        send_d[peer, 0:half_rows, :] = down(dlow_query, peer).astype(BF16)
        query_copy(peer, me).start()
        return 0

    lax.fori_loop(1, n, send_query, 0)
    acc_d[0:half_rows, :] = down(dlow_query, me)

    ret.wait()
    dlow_value = (ADAPTER_SCALE * (dlv_scr[:, 0:tok] + ret_recv[...])).astype(BF16)

    def send_value(k, _):
        peer = lax.rem(me + k, n)
        send_d[peer, half_rows : 2 * half_rows, :] = down(dlow_value, peer).astype(BF16)
        value_copy(peer, me).start()
        return 0

    lax.fori_loop(1, n, send_value, 0)
    acc_d[half_rows : 2 * half_rows, :] = down(dlow_value, me)
    acc_l[...] = send_l[me].astype(F32)

    def gather(k, _):
        src = lax.rem(me + n - k, n)
        lift_copy(src, src).wait_recv()
        acc_l[...] += recv_l[src].astype(F32)
        query_copy(src, src).wait_recv()
        acc_d[0:half_rows, :] += recv_d[src, 0:half_rows, :].astype(F32)
        return 0

    lax.fori_loop(1, n, gather, 0)

    def gather_value(k, _):
        src = lax.rem(me + n - k, n)
        value_copy(src, src).wait_recv()
        acc_d[half_rows : 2 * half_rows, :] += recv_d[src, half_rows : 2 * half_rows, :].astype(F32)
        return 0

    lax.fori_loop(1, n, gather_value, 0)

    whole_d = acc_d[...]
    whole_l = acc_l[...]
    share_d[...] = whole_d.astype(BF16)
    share_l[...] = whole_l.astype(BF16)

    def to_dp(src, dst, ssem, rsem, peer, slot):
        return pltpu.make_async_remote_copy(
            src_ref=src,
            dst_ref=dst.at[slot],
            send_sem=ssem.at[peer],
            recv_sem=rsem.at[slot],
            device_id={"dp": peer},
            device_id_type=MESH,
        )

    def share_d_copy(peer, slot):
        return to_dp(share_d, peer_d, shd_ssem, shd_rsem, peer, slot)

    def share_l_copy(peer, slot):
        return to_dp(share_l, peer_l, shl_ssem, shl_rsem, peer, slot)

    def fac_copy(peer, slot):
        return to_dp(fac_send, fac_recv, fac_ssem, fac_rsem, peer, slot)

    def sq_copy(peer, slot):
        return to_seq(sq_send, sq_recv.at[slot], sq_ssem, sq_rsem, peer, slot)

    squares = jnp.sum(
        jnp.sum(whole_d * whole_d, 0, keepdims=True), 1, keepdims=True
    ) + jnp.sum(jnp.sum(whole_l * whole_l, 0, keepdims=True), 1, keepdims=True)
    sq_send[...] = jnp.broadcast_to(squares, sq_send.shape)

    def send_sq(k, _):
        sq_copy(lax.rem(me + k, n), me).start()
        return 0

    lax.fori_loop(1, n, send_sq, 0)
    for k in range(1, m):
        peer = lax.rem(ex + k, m)
        share_d_copy(peer, ex).start()
        share_l_copy(peer, ex).start()

    def gather_sq(k, total):
        src = lax.rem(me + n - k, n)
        sq_copy(src, src).wait_recv()
        return total + sq_recv[src]

    norm = jnp.sqrt(lax.fori_loop(1, n, gather_sq, sq_send[...]))
    norm_ref[...] = norm
    factor = math.sqrt(PCOUNT) / (norm + STABLE)
    fac_send[...] = factor
    for k in range(1, m):
        fac_copy(lax.rem(ex + k, m), ex).start()

    one = factor[0:1, 0:1]
    sum_d = whole_d * one
    sum_l = whole_l * one
    for k in range(1, m):
        src = lax.rem(ex + m - k, m)
        share_d_copy(src, src).wait_recv()
        share_l_copy(src, src).wait_recv()
        fac_copy(src, src).wait_recv()
        other = fac_recv[src][0:1, 0:1]
        sum_d = sum_d + peer_d[src].astype(F32) * other
        sum_l = sum_l + peer_l[src].astype(F32) * other
    oqd_ref[...] = sum_d[:half_rows] + NOISE_STD * nqd_ref[...]
    ovd_ref[...] = sum_d[half_rows:] + NOISE_STD * nvd_ref[...]
    oql_ref[...] = sum_l[:, 0:wq] + NOISE_STD * nql_ref[...]
    ovl_ref[...] = sum_l[:, wqp : wqp + wv] + NOISE_STD * nvl_ref[...]

    def finish(k, _):
        peer = lax.rem(me + k, n)
        lift_copy(peer, me).wait_send()
        query_copy(peer, me).wait_send()
        value_copy(peer, me).wait_send()
        sq_copy(peer, me).wait_send()
        return 0

    lax.fori_loop(1, n, finish, 0)
    for k in range(1, m):
        peer = lax.rem(ex + k, m)
        share_d_copy(peer, ex).wait_send()
        share_l_copy(peer, ex).wait_send()
        fac_copy(peer, ex).wait_send()


def body(
    n,
    m,
    activations,
    query_states,
    key_states,
    value_states,
    output_grad,
    query_lowrank,
    value_lowrank,
    query_up_matrix,
    value_up_matrix,
    noise_query_down,
    noise_query_lift,
    noise_value_down,
    noise_value_lift,
    block_order,
    valid_lengths,
):
    tok = query_states.shape[1]
    width = activations.shape[2]
    qw = query_states.shape[2]
    kvw = key_states.shape[2]
    rank = query_lowrank.shape[2]
    wd, wq, wv = width // n, qw // n, kvw // n
    wl = max(wq, HEAD) + HEAD
    half = HEAD // 2

    positions = block_order[0, 0] * tok + jnp.arange(tok, dtype=jnp.int32)
    freqs = ROPE_BASE ** (-2.0 * jnp.arange(half).astype(F32) / HEAD)
    freqs = jnp.concatenate([freqs, freqs])
    angle = positions.astype(F32)[:, None] * freqs[None, :]
    signs = jnp.where(jnp.arange(HEAD) < half, -1.0, 1.0).astype(F32)
    cosine = jnp.cos(angle)
    sine = signs[None, :] * jnp.sin(angle)

    vmem = pl.BlockSpec(memory_space=pltpu.VMEM)
    smem = pl.BlockSpec(memory_space=pltpu.SMEM)
    hbm = pl.BlockSpec(memory_space=pl.ANY)
    dma = pltpu.SemaphoreType.DMA
    norm, qd, ql, vd, vl = pl.pallas_call(
        functools.partial(kernel, n, m),
        out_shape=(
            jax.ShapeDtypeStruct((8, HEAD), F32),
            jax.ShapeDtypeStruct((rank, wd), F32),
            jax.ShapeDtypeStruct((rank, wq), F32),
            jax.ShapeDtypeStruct((rank, wd), F32),
            jax.ShapeDtypeStruct((rank, wv), F32),
        ),
        in_specs=[smem, smem, hbm, hbm, hbm] + [vmem] * 12,
        out_specs=(vmem,) * 5,
        scratch_shapes=[
            pltpu.VMEM((tok, qw), BF16),
            pltpu.VMEM((tok, qw), BF16),
            pltpu.VMEM((tok, width), BF16),
            pltpu.VMEM((2 * tok, kvw), BF16),
            pltpu.VMEM((2 * tok, kvw), BF16),
            pltpu.VMEM((rank, tok), BF16),
            pltpu.VMEM((kvw, 2 * tok), BF16),
            pltpu.VMEM((HEAD, tok), F32),
            pltpu.VMEM((HEAD, tok), F32),
            pltpu.VMEM((2 * tok, HEAD), F32),
            pltpu.VMEM((rank, tok), F32),
            pltpu.VMEM((rank, 2 * tok), F32),
            pltpu.VMEM((rank, tok), F32),
            pltpu.VMEM((rank, tok), F32),
            pltpu.VMEM((n, 2 * rank, wd), BF16),
            pltpu.VMEM((n, 2 * rank, wd), BF16),
            pltpu.VMEM((n, rank, wl), BF16),
            pltpu.VMEM((n, rank, wl), BF16),
            pltpu.VMEM((2 * rank, wd), F32),
            pltpu.VMEM((rank, wl), F32),
            pltpu.VMEM((2 * rank, wd), BF16),
            pltpu.VMEM((rank, wl), BF16),
            pltpu.VMEM((m, 2 * rank, wd), BF16),
            pltpu.VMEM((m, rank, wl), BF16),
            pltpu.VMEM((8, HEAD), F32),
            pltpu.VMEM((n, 8, HEAD), F32),
            pltpu.VMEM((8, HEAD), F32),
            pltpu.VMEM((m, 8, HEAD), F32),
            dma((3,)),
            dma((3,)),
            dma((3,)),
            dma,
            dma,
        ]
        + [dma((n,))] * 8
        + [dma((m,))] * 6,
        compiler_params=pltpu.CompilerParams(
            collective_id=0, has_side_effects=True, vmem_limit_bytes=48 * 1024 * 1024
        ),
        name="adapter_backward",
    )(
        block_order,
        valid_lengths,
        query_states[0],
        output_grad[0],
        activations[0],
        key_states[0],
        value_states[0],
        cosine,
        sine,
        query_lowrank[0].T,
        value_lowrank[0].T,
        query_up_matrix,
        value_up_matrix,
        noise_query_down.T,
        noise_query_lift,
        noise_value_down.T,
        noise_value_lift,
    )
    return (norm[0, 0:1], qd.T, ql, vd.T, vl)


def solution(mesh):
    in_specs = (
        P("dp", "seq", None),
        P("dp", "seq", None),
        P("dp", "seq", None),
        P("dp", "seq", None),
        P("dp", "seq", None),
        P("dp", "seq", None),
        P("dp", "seq", None),
        P(),
        P(),
        P("seq", None),
        P(None, "seq"),
        P("seq", None),
        P(None, "seq"),
        P("dp", "seq"),
        P("dp"),
    )
    out_specs = (P("dp"), P("seq", None), P(None, "seq"), P("seq", None), P(None, "seq"))
    inner = functools.partial(body, mesh.shape["seq"], mesh.shape["dp"])
    return jax.shard_map(inner, mesh=mesh, in_specs=in_specs, out_specs=out_specs, check_vma=False)
```

time: 261 us -> 88.8 us (0.34)
  waiting for transfers between devices: 76.5 us -> 0 us
  Pallas kernels: 0 us -> 71.3 us
  blocking collectives: 50.3 us -> 0 us
  matrix products: 46.2 us -> 0 us
  other arithmetic: 33.1 us -> 0.63 us
  between operations: 20 us -> 1.97 us
  local copies, waits for them, and re-layouts: 23.7 us -> 14.2 us
  starting transfers between devices: 9.45 us -> 0 us
    psum x2 -> x0, waiting for transfers between devices: 76.3 us -> none  [the longest x1 46.8 us: body(): lax.psum((grad_query_down, query_upward_gradient, grad_value_down, value_...]
    pallas_call x0 -> x1, Pallas kernels: none -> 71.3 us  [body(): pl.pallas_call(functools.partial(kernel, n, m), out_shape=(jax.ShapeDtype...]
    psum x2 -> x0, blocking collectives: 50.3 us -> none  [the longest x1 38.7 us: body(): lax.psum((grad_query_down, query_upward_gradient, grad_value_down, value_...]
    dot_general x20 -> x0, matrix products: 46.2 us -> none  [the longest x4 17.2 us: one_head(): jnp.einsum('gtk,kd->tgd', dscore, key_head, preferred_element_type=jnp.fl...]
    sub x5 -> x0, other arithmetic: 10.3 us -> none  [the longest x4 7.39 us: one_head(): shifted = jnp.exp(scores - row_max)]
    ppermute x4 -> x0, starting transfers between devices: 9.37 us -> none  [from_behind(): lax.ppermute(array, axis, [(i, (i + by) % devices) for i in range(devices)])]
    unnamed x22 -> x28, local copies, waits for them, and re-layouts: 5.9 us -> 13.7 us
    while x16 -> x0, local copies, waits for them, and re-layouts: 6.34 us -> none
  transfers between devices with their start and end apart: 6 -> 0, of which waited for: 3 -> 0; matrix products, arithmetic and copies ran while one was open for 12% -> 0% of each run, Pallas kernels for 0% -> 0%
where the time goes in v1:
time: 88.8 us; the launch traced here: 88.2 us
  Pallas kernels  71.3 us (80%)
  local copies, waits for them, and re-layouts  14.2 us (16%)
  between operations  1.97 us (2%)
    pallas_call x1, Pallas kernels, body(): pl.pallas_call(functools.partial(kernel, n, m), out_shape=(jax.ShapeDtype...  71.3 us
    unnamed x28, local copies, waits for them, and re-layouts  13.7 us

profile of v1, /device:TPU:0, one launch (start us, length us, event | category | flops | bytes accessed | tf_op | source)
XLA Modules:
  0.0 88.2 jit_solution(14496184124373092157)
XLA Ops:
  1.9 0.1 compare_select_fusion
  2.0 0.5 fusion
  2.6 0.0 copy-start
  2.6 1.6 %copy-done = bf16[1,256,4096]{2,1,0:T(8,128)(2,1)S(1)} copy-done((bf16[1,256,4096]{2,1,0:T(8,128)(2,1)S(1)}, bf16[1,256,4096]{2,1,0:T(8,128)(2,1)}, u32[]{:S(2)}) %copy-start) | copy-done | bytes 2097176
  4.2 0.0 copy-start.1
  4.2 1.6 %copy-done.1 = bf16[1,256,4096]{2,1,0:T(8,128)(2,1)S(1)} copy-done((bf16[1,256,4096]{2,1,0:T(8,128)(2,1)S(1)}, bf16[1,256,4096]{2,1,0:T(8,128)(2,1)}, u32[]{:S(2)}) %copy-start.1) | copy-done | bytes 2097176
  5.8 0.0 copy-start.2
  5.8 0.9 %copy-done.2 = bf16[1,256,512]{2,1,0:T(8,128)(2,1)S(1)} copy-done((bf16[1,256,512]{2,1,0:T(8,128)(2,1)S(1)}, bf16[1,256,512]{2,1,0:T(8,128)(2,1)}, u32[]{:S(2)}) %copy-start.2) | copy-done | bytes 262168
  6.7 0.0 copy-start.3
  6.7 0.9 %copy-done.3 = bf16[1,256,512]{2,1,0:T(8,128)(2,1)S(1)} copy-done((bf16[1,256,512]{2,1,0:T(8,128)(2,1)S(1)}, bf16[1,256,512]{2,1,0:T(8,128)(2,1)}, u32[]{:S(2)}) %copy-start.3) | copy-done | bytes 262168
  7.7 0.0 copy-start.4
  7.7 0.9 %copy-done.4 = bf16[16,4096]{1,0:T(8,128)(2,1)S(1)} copy-done((bf16[16,4096]{1,0:T(8,128)(2,1)S(1)}, bf16[16,4096]{1,0:T(8,128)(2,1)}, u32[]{:S(2)}) %copy-start.4) | copy-done | bytes 131096
  8.6 0.0 copy-start.5
  8.6 0.8 copy-done.5
  9.4 0.0 copy-start.6
  9.4 0.8 copy-done.6
  10.2 0.0 copy-start.7
  10.2 0.8 copy-done.7
  11.0 0.0 copy-start.8
  11.0 0.7 copy-done.8
  11.7 0.0 copy-start.9
  11.7 0.7 copy-done.9
  12.4 0.0 copy-start.10
  12.4 0.7 copy-done.10
  13.1 0.0 copy-start.11
  13.1 0.7 copy-done.11
  13.8 71.3 %adapter_backward.1 = (f32[8,128]{1,0:T(8,128)S(1)}, f32[16,1024]{1,0:T(8,128)S(1)}, f32[16,512]{1,0:T(8,128)S(1)}, f32[16,1024]{1,0:T(8,128)S(1)}, f32[16,64]{1,0:T(8,128)S(1)}) custom-call(s32[1,1]{1,0:T(1,128)S(6)} %copy.24.order_ref, s32[1]{0:T(128)S(6)} %copy.25.valid_ref, bf16[256,4096]{1,0:T(8,128)(2,1)S(1)} %bitcast.17, ...), custom_call_target="tpu_custom_call" | custom-call | tf_op jit(solution)/shard_map/adapter_backward/pallas_call | solution.py:496
  85.2 0.5 slice.3
  85.7 0.6 copy.26
  86.3 0.6 copy.27
  86.9 0.6 copy.28
  87.6 0.6 copy.29
  (2 shorter events, 0.0 us)
Async XLA Ops:
  2.6 1.6 %copy-start = (bf16[1,256,4096]{2,1,0:T(8,128)(2,1)S(1)}, bf16[1,256,4096]{2,1,0:T(8,128)(2,1)}, u32[]{:S(2)}) copy-start(bf16[1,256,4096]{2,1,0:T(8,128)(2,1)} %param.16) | copy-start | bytes 6291460
  4.2 1.6 %copy-start.1 = (bf16[1,256,4096]{2,1,0:T(8,128)(2,1)S(1)}, bf16[1,256,4096]{2,1,0:T(8,128)(2,1)}, u32[]{:S(2)}) copy-start(bf16[1,256,4096]{2,1,0:T(8,128)(2,1)} %param.19) | copy-start | bytes 6291460
  5.8 0.9 %copy-start.2 = (bf16[1,256,512]{2,1,0:T(8,128)(2,1)S(1)}, bf16[1,256,512]{2,1,0:T(8,128)(2,1)}, u32[]{:S(2)}) copy-start(bf16[1,256,512]{2,1,0:T(8,128)(2,1)} %param.17) | copy-start | bytes 786436
  6.7 0.9 %copy-start.3 = (bf16[1,256,512]{2,1,0:T(8,128)(2,1)S(1)}, bf16[1,256,512]{2,1,0:T(8,128)(2,1)}, u32[]{:S(2)}) copy-start(bf16[1,256,512]{2,1,0:T(8,128)(2,1)} %param.18) | copy-start | bytes 786436
  7.7 0.9 %copy-start.4 = (bf16[16,4096]{1,0:T(8,128)(2,1)S(1)}, bf16[16,4096]{1,0:T(8,128)(2,1)}, u32[]{:S(2)}) copy-start(bf16[16,4096]{1,0:T(8,128)(2,1)} %qup_ref.1) | copy-start | bytes 393220
  8.6 0.8 copy-start.5
  9.4 0.8 copy-start.6
  10.2 0.8 copy-start.7
  11.0 0.7 copy-start.8
  11.7 0.7 copy-start.9
  12.4 0.7 copy-start.10
  13.1 0.7 copy-start.11

commit v2 on v1

--- a/solution.py
+++ b/solution.py
@@ -45,10 +45,27 @@
     q_hbm,
     g_hbm,
     acts_hbm,
-    k_ref,
-    v_ref,
+    k_hbm,
+    v_hbm,
     cos_ref,
     sin_ref,
+    qlt_hbm,
+    vlt_hbm,
+    qup_hbm,
+    vup_hbm,
+    nqd_hbm,
+    nql_hbm,
+    nvd_hbm,
+    nvl_hbm,
+    norm_ref,
+    oqd_ref,
+    oql_ref,
+    ovd_ref,
+    ovl_ref,
+    q_scr,
+    g_scr,
+    acts_scr,
+    k_ref,
     qlt_ref,
     vlt_ref,
     qup_ref,
@@ -57,14 +74,6 @@
     nql_ref,
     nvd_ref,
     nvl_ref,
-    norm_ref,
-    oqd_ref,
-    oql_ref,
-    ovd_ref,
-    ovl_ref,
-    q_scr,
-    g_scr,
-    acts_scr,
     kwin,
     vwin,
     vlt_prev,
@@ -76,9 +85,13 @@
     dlv_scr,
     ret_send,
     ret_recv,
+    pair_d,
+    got_d,
     send_d,
     recv_d,
     send_l,
+    got_l,
+    pair_l,
     recv_l,
     acc_d,
     acc_l,
@@ -95,12 +108,18 @@
     halo_rsem,
     ret_ssem,
     ret_rsem,
-    l_ssem,
-    l_rsem,
-    dq_ssem,
-    dq_rsem,
-    dv_ssem,
-    dv_rsem,
+    l1_ssem,
+    l1_rsem,
+    l2_ssem,
+    l2_rsem,
+    q1_ssem,
+    q1_rsem,
+    q2_ssem,
+    q2_rsem,
+    v1_ssem,
+    v1_rsem,
+    v2_ssem,
+    v2_rsem,
     sq_ssem,
     sq_rsem,
     shd_ssem,
@@ -112,6 +131,10 @@
 ):
     me = lax.axis_index("seq")
     ex = lax.axis_index("dp")
+    side = lax.rem(me, 2)
+    depth = me // 2
+    nz = n // 2
+    partner = me + 1 - 2 * side
     right = lax.rem(me + 1, n)
     left = lax.rem(me + n - 1, n)
     tok = k_ref.shape[0]
@@ -124,12 +147,29 @@
     scaling = 1.0 / math.sqrt(HEAD)
     c2 = scaling * math.log2(math.e)
 
-    load_q = pltpu.make_async_copy(q_hbm, q_scr, local_sem.at[0])
-    load_g = pltpu.make_async_copy(g_hbm, g_scr, local_sem.at[1])
-    load_acts = pltpu.make_async_copy(acts_hbm, acts_scr, local_sem.at[2])
-    load_q.start()
-    load_g.start()
-    load_acts.start()
+    def load(i, src, dst):
+        copy = pltpu.make_async_copy(src, dst, local_sem.at[i])
+        copy.start()
+        return copy
+
+    load_k = load(0, k_hbm, k_ref)
+    load_q = load(3, q_hbm, q_scr)
+    load_v = [
+        load(4 + c, v_hbm.at[:, pl.ds(c * HEAD, HEAD)], vwin.at[c, pl.ds(0, tok)])
+        for c in range(groups)
+    ]
+    load_g = load(8, g_hbm, g_scr)
+    load_small = [
+        load(9, qlt_hbm, qlt_ref),
+        load(10, vlt_hbm, vlt_ref),
+        load(11, qup_hbm, qup_ref),
+        load(12, vup_hbm, vup_ref),
+        load(13, nqd_hbm, nqd_ref),
+        load(14, nql_hbm, nql_ref),
+        load(15, nvd_hbm, nvd_ref),
+        load(16, nvl_hbm, nvl_ref),
+    ]
+    load_acts = load(17, acts_hbm, acts_scr)
 
     barrier = pltpu.get_barrier_semaphore()
 
@@ -143,14 +183,13 @@
         peer = lax.rem(ex + k, m)
         pl.semaphore_signal(barrier, inc=1, device_id={"dp": peer}, device_id_type=MESH)
 
+    load_k.wait()
     cos = cos_ref[...]
     sin = sin_ref[...]
     for c in range(groups):
-        cols = slice(c * HEAD, (c + 1) * HEAD)
-        k = k_ref[:, cols].astype(F32)
+        k = k_ref[:, c * HEAD : (c + 1) * HEAD].astype(F32)
         kr = k * cos + pltpu.roll(k, HEAD // 2, 1) * sin
-        kwin[0:tok, cols] = kr.astype(BF16)
-        kt_scr[cols, 0:tok] = kr.T.astype(BF16)
+        kwin[c, 0:tok, :] = kr.astype(BF16)
     pl.semaphore_wait(barrier, n - 1 + m - 1)
 
     def halo(i, src, dst):
@@ -163,14 +202,22 @@
             device_id_type=MESH,
         )
 
-    halos = [
-        halo(0, kwin.at[pl.ds(0, tok)], kwin.at[pl.ds(tok, tok)]),
-        halo(1, v_ref, vwin.at[pl.ds(tok, tok)]),
-        halo(2, vlt_ref, vlt_prev),
-    ]
-    for h in halos:
-        h.start()
-    vwin[0:tok, :] = v_ref[...]
+    def key_halo(c):
+        return halo(2 * c, kwin.at[c, pl.ds(0, tok)], kwin.at[c, pl.ds(tok, tok)])
+
+    def value_halo(c):
+        return halo(2 * c + 1, v_hbm.at[:, pl.ds(c * HEAD, HEAD)], vwin.at[c, pl.ds(tok, tok)])
+
+    lowrank_halo = halo(2 * groups, vlt_hbm, vlt_prev)
+    for c in range(groups):
+        key_halo(c).start()
+        value_halo(c).start()
+        if c == 0:
+            lowrank_halo.start()
+    for c in range(groups):
+        k = k_ref[:, c * HEAD : (c + 1) * HEAD].astype(F32)
+        kr = k * cos + pltpu.roll(k, HEAD // 2, 1) * sin
+        kt_scr[c, :, 0:tok] = kr.T.astype(BF16)
     cost_scr[...] = cos.T
     sint_scr[...] = sin.T
     send_l[...] = jnp.zeros_like(send_l)
@@ -193,11 +240,9 @@
 
     lax.fori_loop(0, groups * heads, rope_queries, 0, unroll=4)
     load_g.wait()
-    for h in halos:
-        h.wait()
-    for c in range(groups):
-        cols = slice(c * HEAD, (c + 1) * HEAD)
-        kt_scr[cols, tok : 2 * tok] = kwin[tok : 2 * tok, cols].astype(F32).T.astype(BF16)
+    for copy in load_v + load_small:
+        copy.wait()
+    lowrank_halo.wait()
 
     key_at = lax.broadcasted_iota(jnp.int32, (tok, tok), 0)
     row_at = lax.broadcasted_iota(jnp.int32, (tok, tok), 1)
@@ -205,11 +250,10 @@
 
     def one_head(c, i):
         h = c * heads + i
-        kcols = pl.ds(pl.multiple_of(c * HEAD, HEAD), HEAD)
         cols = pl.ds(pl.multiple_of(h * HEAD, HEAD), HEAD)
         qr = q_scr[:, cols]
         g = g_scr[:, cols] * keep
-        s = dot_nt(kwin[:, kcols], qr)
+        s = dot_nt(kwin[c], qr)
         own = jnp.where(causal, s[:tok], NEG)
         prev = s[tok:]
         top = jnp.maximum(
@@ -219,12 +263,14 @@
         e_own = jnp.exp2(own * c2 - shift)
         e_prev = jnp.exp2(prev * c2 - (shift - bias))
         total = jnp.sum(e_own, 0, keepdims=True) + jnp.sum(e_prev, 0, keepdims=True)
-        p = jnp.concatenate([e_own, e_prev], 0) * (1.0 / total)
-        dp = dot_nt(vwin[:, kcols], g)
-        delta = jnp.sum(p * dp, 0, keepdims=True)
+        e = jnp.concatenate([e_own, e_prev], 0)
+        inverse = 1.0 / total
+        dp = dot_nt(vwin[c], g)
+        delta = jnp.sum(e * dp, 0, keepdims=True) * inverse
+        p = e * inverse
         ds = (p * (dp - delta)).astype(BF16)
         dv = dot(p.astype(BF16), g)
-        dq = dot(kt_scr[kcols, :], ds) * scaling
+        dq = dot(kt_scr[c], ds) * scaling
         half = HEAD // 2
         swapped = jnp.concatenate([dq[half:], dq[:half]], 0)
         dq_low = (dq * cost_scr[...] - swapped * sint_scr[...]).astype(BF16)
@@ -240,10 +286,28 @@
                 send_l[h * per + j, :, 0:HEAD] = lane_piece(lift, j, wq).astype(BF16)
         return dv, dlq
 
-    unroll = 4
+    def to_seq(src, dst, ssem, rsem, peer):
+        return pltpu.make_async_remote_copy(
+            src_ref=src,
+            dst_ref=dst,
+            send_sem=ssem,
+            recv_sem=rsem,
+            device_id={"seq": peer},
+            device_id_type=MESH,
+        )
+
+    def lift_pair(z):
+        return to_seq(
+            send_l.at[2 * z + 1 - side], got_l.at[z], l1_ssem.at[z], l1_rsem.at[z], partner
+        )
+
+    unroll = 8
 
     def one_group(c, _):
         dv_scr[...] = jnp.zeros_like(dv_scr)
+        key_halo(c).wait()
+        value_halo(c).wait()
+        kt_scr[c, :, tok : 2 * tok] = kwin[c, tok : 2 * tok, :].astype(F32).T.astype(BF16)
 
         def some_heads(step, _):
             dvs = None
@@ -265,6 +329,9 @@
         per = HEAD // wv
         for j in range(per):
             send_l[c * per + j, :, wqp : wqp + HEAD] = lane_piece(vlift, j, wv).astype(BF16)
+        per = nz // groups
+        for j in range(per):
+            lift_pair(c * per + j).start()
         return 0
 
     lax.fori_loop(0, groups, one_group, 0)
@@ -280,46 +347,29 @@
     )
     ret.start()
 
-    def to_seq(src, dst, ssem, rsem, peer, slot):
-        return pltpu.make_async_remote_copy(
-            src_ref=src,
-            dst_ref=dst,
-            send_sem=ssem.at[peer],
-            recv_sem=rsem.at[slot],
-            device_id={"seq": peer},
-            device_id_type=MESH,
+    def lift_copy(z, at):
+        return to_seq(
+            pair_l.at[z], recv_l.at[at], l2_ssem.at[z], l2_rsem.at[at], 2 * z + side
         )
 
-    def lift_copy(peer, slot):
-        return to_seq(send_l.at[peer], recv_l.at[slot], l_ssem, l_rsem, peer, slot)
-
     half_rows = qlt_ref.shape[0]
-
-    def query_copy(peer, slot):
-        return to_seq(
-            send_d.at[peer, pl.ds(0, half_rows)],
-            recv_d.at[slot, pl.ds(0, half_rows)],
-            dq_ssem,
-            dq_rsem,
-            peer,
-            slot,
+    upper = pl.ds(0, half_rows)
+    lower = pl.ds(half_rows, half_rows)
+
+    def down_pair(part, ssem, rsem):
+        return lambda z: to_seq(
+            pair_d.at[z, part], got_d.at[z, part], ssem.at[z], rsem.at[z], partner
         )
 
-    def value_copy(peer, slot):
-        return to_seq(
-            send_d.at[peer, pl.ds(half_rows, half_rows)],
-            recv_d.at[slot, pl.ds(half_rows, half_rows)],
-            dv_ssem,
-            dv_rsem,
-            peer,
-            slot,
+    def down_copy(part, ssem, rsem):
+        return lambda z, at: to_seq(
+            send_d.at[z, part], recv_d.at[at, part], ssem.at[z], rsem.at[at], 2 * z + side
         )
 
-    def send_lift(k, _):
-        lift_copy(lax.rem(me + k, n), me).start()
-        return 0
-
-    lax.fori_loop(1, n, send_lift, 0)
+    query_pair = down_pair(upper, q1_ssem, q1_rsem)
+    value_pair = down_pair(lower, v1_ssem, v1_rsem)
+    query_copy = down_copy(upper, q2_ssem, q2_rsem)
+    value_copy = down_copy(lower, v2_ssem, v2_rsem)
 
     load_acts.wait()
     dlow_query = (ADAPTER_SCALE * dlq_scr[...]).astype(BF16)
@@ -327,45 +377,79 @@
     def down(low, slot):
         return dot(low, acts_scr[:, pl.ds(pl.multiple_of(slot * wd, wd), wd)])
 
-    def send_query(k, _):
-        peer = lax.rem(me + k, n)
-        send_d[peer, 0:half_rows, :] = down(dlow_query, peer).astype(BF16)
-        query_copy(peer, me).start()
-        return 0
-
-    lax.fori_loop(1, n, send_query, 0)
-    acc_d[0:half_rows, :] = down(dlow_query, me)
+    def pair_query(k, _):
+        z = lax.rem(depth + k, nz)
+        pair_d[z, 0:half_rows, :] = down(dlow_query, 2 * z + 1 - side).astype(BF16)
+        query_pair(z).start()
+        return 0
+
+    lax.fori_loop(1, nz + 1, pair_query, 0)
+
+    def send_lift(k, _):
+        z = lax.rem(depth + k, nz)
+        lift_pair(z).wait_recv()
+        pair_l[z] = (send_l[2 * z + side].astype(F32) + got_l[z].astype(F32)).astype(BF16)
+        lift_copy(z, depth).start()
+        return 0
+
+    lax.fori_loop(1, nz, send_lift, 0)
+    lift_pair(depth).wait_recv()
+    acc_l[...] = send_l[me].astype(F32) + got_l[depth].astype(F32)
 
     ret.wait()
     dlow_value = (ADAPTER_SCALE * (dlv_scr[:, 0:tok] + ret_recv[...])).astype(BF16)
 
+    def pair_value(k, _):
+        z = lax.rem(depth + k, nz)
+        pair_d[z, half_rows : 2 * half_rows, :] = down(dlow_value, 2 * z + 1 - side).astype(BF16)
+        value_pair(z).start()
+        return 0
+
+    lax.fori_loop(1, nz + 1, pair_value, 0)
+
+    def send_query(k, _):
+        z = lax.rem(depth + k, nz)
+        own = down(dlow_query, 2 * z + side)
+        query_pair(z).wait_recv()
+        send_d[z, 0:half_rows, :] = (own + got_d[z, 0:half_rows, :].astype(F32)).astype(BF16)
+        query_copy(z, depth).start()
+        return 0
+
+    lax.fori_loop(1, nz, send_query, 0)
+
     def send_value(k, _):
-        peer = lax.rem(me + k, n)
-        send_d[peer, half_rows : 2 * half_rows, :] = down(dlow_value, peer).astype(BF16)
-        value_copy(peer, me).start()
-        return 0
-
-    lax.fori_loop(1, n, send_value, 0)
+        z = lax.rem(depth + k, nz)
+        own = down(dlow_value, 2 * z + side)
+        value_pair(z).wait_recv()
+        got = got_d[z, half_rows : 2 * half_rows, :].astype(F32)
+        send_d[z, half_rows : 2 * half_rows, :] = (own + got).astype(BF16)
+        value_copy(z, depth).start()
+        return 0
+
+    lax.fori_loop(1, nz, send_value, 0)
+    acc_d[0:half_rows, :] = down(dlow_query, me)
     acc_d[half_rows : 2 * half_rows, :] = down(dlow_value, me)
-    acc_l[...] = send_l[me].astype(F32)
+    query_pair(depth).wait_recv()
+    value_pair(depth).wait_recv()
+    acc_d[...] += got_d[depth].astype(F32)
 
     def gather(k, _):
-        src = lax.rem(me + n - k, n)
-        lift_copy(src, src).wait_recv()
-        acc_l[...] += recv_l[src].astype(F32)
-        query_copy(src, src).wait_recv()
-        acc_d[0:half_rows, :] += recv_d[src, 0:half_rows, :].astype(F32)
-        return 0
-
-    lax.fori_loop(1, n, gather, 0)
+        z = lax.rem(depth + nz - k, nz)
+        lift_copy(z, z).wait_recv()
+        acc_l[...] += recv_l[z].astype(F32)
+        query_copy(z, z).wait_recv()
+        acc_d[0:half_rows, :] += recv_d[z, 0:half_rows, :].astype(F32)
+        return 0
+
+    lax.fori_loop(1, nz, gather, 0)
 
     def gather_value(k, _):
-        src = lax.rem(me + n - k, n)
-        value_copy(src, src).wait_recv()
-        acc_d[half_rows : 2 * half_rows, :] += recv_d[src, half_rows : 2 * half_rows, :].astype(F32)
-        return 0
-
-    lax.fori_loop(1, n, gather_value, 0)
+        z = lax.rem(depth + nz - k, nz)
+        value_copy(z, z).wait_recv()
+        acc_d[half_rows : 2 * half_rows, :] += recv_d[z, half_rows : 2 * half_rows, :].astype(F32)
+        return 0
+
+    lax.fori_loop(1, nz, gather_value, 0)
 
     whole_d = acc_d[...]
     whole_l = acc_l[...]
@@ -392,7 +476,7 @@
         return to_dp(fac_send, fac_recv, fac_ssem, fac_rsem, peer, slot)
 
     def sq_copy(peer, slot):
-        return to_seq(sq_send, sq_recv.at[slot], sq_ssem, sq_rsem, peer, slot)
+        return to_seq(sq_send, sq_recv.at[slot], sq_ssem.at[peer], sq_rsem.at[slot], peer)
 
     squares = jnp.sum(
         jnp.sum(whole_d * whole_d, 0, keepdims=True), 1, keepdims=True
@@ -437,15 +521,28 @@
     oql_ref[...] = sum_l[:, 0:wq] + NOISE_STD * nql_ref[...]
     ovl_ref[...] = sum_l[:, wqp : wqp + wv] + NOISE_STD * nvl_ref[...]
 
-    def finish(k, _):
-        peer = lax.rem(me + k, n)
-        lift_copy(peer, me).wait_send()
-        query_copy(peer, me).wait_send()
-        value_copy(peer, me).wait_send()
-        sq_copy(peer, me).wait_send()
-        return 0
-
-    lax.fori_loop(1, n, finish, 0)
+    def finish_sq(k, _):
+        sq_copy(lax.rem(me + k, n), me).wait_send()
+        return 0
+
+    lax.fori_loop(1, n, finish_sq, 0)
+
+    def finish_pair(z, _):
+        lift_pair(z).wait_send()
+        query_pair(z).wait_send()
+        value_pair(z).wait_send()
+        return 0
+
+    lax.fori_loop(0, nz, finish_pair, 0)
+
+    def finish_copy(k, _):
+        z = lax.rem(depth + k, nz)
+        lift_copy(z, depth).wait_send()
+        query_copy(z, depth).wait_send()
+        value_copy(z, depth).wait_send()
+        return 0
+
+    lax.fori_loop(1, nz, finish_copy, 0)
     for k in range(1, m):
         peer = lax.rem(ex + k, m)
         share_d_copy(peer, ex).wait_send()
@@ -479,6 +576,8 @@
     rank = query_lowrank.shape[2]
     wd, wq, wv = width // n, qw // n, kvw // n
     wl = max(wq, HEAD) + HEAD
+    groups = kvw // HEAD
+    nz = n // 2
     half = HEAD // 2
 
     positions = block_order[0, 0] * tok + jnp.arange(tok, dtype=jnp.int32)
@@ -491,7 +590,7 @@
 
     vmem = pl.BlockSpec(memory_space=pltpu.VMEM)
     smem = pl.BlockSpec(memory_space=pltpu.SMEM)
-    hbm = pl.BlockSpec(memory_space=pl.ANY)
+    hbm = pl.BlockSpec(memory_space=pltpu.HBM)
     dma = pltpu.SemaphoreType.DMA
     norm, qd, ql, vd, vl = pl.pallas_call(
         functools.partial(kernel, n, m),
@@ -502,16 +601,25 @@
             jax.ShapeDtypeStruct((rank, wd), F32),
             jax.ShapeDtypeStruct((rank, wv), F32),
         ),
-        in_specs=[smem, smem, hbm, hbm, hbm] + [vmem] * 12,
+        in_specs=[smem, smem] + [hbm] * 5 + [vmem] * 2 + [hbm] * 8,
         out_specs=(vmem,) * 5,
         scratch_shapes=[
             pltpu.VMEM((tok, qw), BF16),
             pltpu.VMEM((tok, qw), BF16),
             pltpu.VMEM((tok, width), BF16),
-            pltpu.VMEM((2 * tok, kvw), BF16),
-            pltpu.VMEM((2 * tok, kvw), BF16),
+            pltpu.VMEM((tok, kvw), BF16),
             pltpu.VMEM((rank, tok), BF16),
-            pltpu.VMEM((kvw, 2 * tok), BF16),
+            pltpu.VMEM((rank, tok), BF16),
+            pltpu.VMEM((rank, qw), BF16),
+            pltpu.VMEM((rank, kvw), BF16),
+            pltpu.VMEM((rank, wd), F32),
+            pltpu.VMEM((rank, wq), F32),
+            pltpu.VMEM((rank, wd), F32),
+            pltpu.VMEM((rank, wv), F32),
+            pltpu.VMEM((groups, 2 * tok, HEAD), BF16),
+            pltpu.VMEM((groups, 2 * tok, HEAD), BF16),
+            pltpu.VMEM((rank, tok), BF16),
+            pltpu.VMEM((groups, HEAD, 2 * tok), BF16),
             pltpu.VMEM((HEAD, tok), F32),
             pltpu.VMEM((HEAD, tok), F32),
             pltpu.VMEM((2 * tok, HEAD), F32),
@@ -519,10 +627,14 @@
             pltpu.VMEM((rank, 2 * tok), F32),
             pltpu.VMEM((rank, tok), F32),
             pltpu.VMEM((rank, tok), F32),
-            pltpu.VMEM((n, 2 * rank, wd), BF16),
-            pltpu.VMEM((n, 2 * rank, wd), BF16),
+            pltpu.VMEM((nz, 2 * rank, wd), BF16),
+            pltpu.VMEM((nz, 2 * rank, wd), BF16),
+            pltpu.VMEM((nz, 2 * rank, wd), BF16),
+            pltpu.VMEM((nz, 2 * rank, wd), BF16),
             pltpu.VMEM((n, rank, wl), BF16),
-            pltpu.VMEM((n, rank, wl), BF16),
+            pltpu.VMEM((nz, rank, wl), BF16),
+            pltpu.VMEM((nz, rank, wl), BF16),
+            pltpu.VMEM((nz, rank, wl), BF16),
             pltpu.VMEM((2 * rank, wd), F32),
             pltpu.VMEM((rank, wl), F32),
             pltpu.VMEM((2 * rank, wd), BF16),
@@ -533,16 +645,17 @@
             pltpu.VMEM((n, 8, HEAD), F32),
             pltpu.VMEM((8, HEAD), F32),
             pltpu.VMEM((m, 8, HEAD), F32),
-            dma((3,)),
-            dma((3,)),
-            dma((3,)),
+            dma((18,)),
+            dma((2 * groups + 1,)),
+            dma((2 * groups + 1,)),
             dma,
             dma,
         ]
-        + [dma((n,))] * 8
+        + [dma((nz,))] * 12
+        + [dma((n,))] * 2
         + [dma((m,))] * 6,
         compiler_params=pltpu.CompilerParams(
-            collective_id=0, has_side_effects=True, vmem_limit_bytes=48 * 1024 * 1024
+            collective_id=0, has_side_effects=True, vmem_limit_bytes=60 * 1024 * 1024
         ),
         name="adapter_backward",
     )(

time: 88.8 us -> 67.4 us (0.76)
  Pallas kernels: 71.3 us -> 56.9 us
  local copies, waits for them, and re-layouts: 14.2 us -> 6.81 us
    pallas_call x1, Pallas kernels: 71.3 us -> 56.9 us  [body(): pl.pallas_call(functools.partial(kernel, n, m), out_shape=(jax.ShapeDtype...]
    unnamed x28 -> x4, local copies, waits for them, and re-layouts: 13.7 us -> 5.61 us
where the time goes in v2:
time: 67.4 us; the launch traced here: 67 us
  Pallas kernels  56.9 us (84%)
  local copies, waits for them, and re-layouts  6.81 us (10%)
  between operations  1.95 us (3%)
  other arithmetic  1.33 us (2%)
    pallas_call x1, Pallas kernels, body(): pl.pallas_call(functools.partial(kernel, n, m), out_shape=(jax.ShapeDtype...  56.9 us
    unnamed x4, local copies, waits for them, and re-layouts  5.61 us

profile of v2, /device:TPU:0, one launch (start us, length us, event | category | flops | bytes accessed | tf_op | source)
XLA Modules:
  0.0 67.0 jit_solution(5951776150396837953)
XLA Ops:
  1.9 0.1 compare_select_fusion
  2.0 1.2 %fusion = (f32[256,128]{1,0:T(8,128)}, f32[256,128]{1,0:T(8,128)}) fusion(f32[128]{0:T(128)S(1)} %get-tuple-element.17, f32[128]{0:T(128)S(1)} %get-tuple-element.18, f32[256]{0:T(256)S(1)} %add_convert_fusion), kind=kLoop, calls=%fused_computation.2 | loop fusion | flops 65536 | bytes 264192 | tf_op jit(solution)/shard_map/mul | solution.py:589
  3.3 56.9 %adapter_backward.1 = (f32[8,128]{1,0:T(8,128)}, f32[16,1024]{1,0:T(8,128)}, f32[16,512]{1,0:T(8,128)}, f32[16,1024]{1,0:T(8,128)}, f32[16,64]{1,0:T(8,128)}) custom-call(s32[1,1]{1,0:T(1,128)S(6)} %copy.24.order_ref, s32[1]{0:T(128)S(6)} %copy.25.valid_ref, bf16[256,4096]{1,0:T(8,128)(2,1)} %bitcast.18, bf16[256,4096]{1,0:T(8,128)(2,1)} %bitcast.19, ...), custom_call_target="tpu_custom_call" | custom-call | tf_op jit(solution)/shard_map/adapter_backward/pallas_call | solution.py:595
  60.2 1.2 %slice.3 = f32[1,1]{1,0:T(1,128)} slice(f32[8,128]{1,0:T(8,128)} %get-tuple-element.10), slice={[0:1], [0:1]} | slice | bytes 8 | tf_op jit(solution)/shard_map/slice | solution.py:680
  61.4 1.5 %copy.26 = f32[1024,16]{0,1:T(8,128)} copy(f32[1024,16]{0,1:T(8,128)} %bitcast.25) | data formatting | bytes 131072
  62.9 1.4 %copy.27 = f32[16,512]{1,0:T(8,128)} copy(f32[16,512]{1,0:T(8,128)} %get-tuple-element.26) | data formatting | bytes 65536
  64.3 1.5 %copy.28 = f32[1024,16]{0,1:T(8,128)} copy(f32[1024,16]{0,1:T(8,128)} %bitcast.24) | data formatting | bytes 131072
  65.7 1.3 %copy.29 = f32[16,64]{1,0:T(8,128)} copy(f32[16,64]{1,0:T(8,128)} %get-tuple-element.28) | data formatting | bytes 8192
  (2 shorter events, 0.0 us)

commit v3 on v2

--- a/solution.py
+++ b/solution.py
@@ -57,11 +57,7 @@
     nql_hbm,
     nvd_hbm,
     nvl_hbm,
-    norm_ref,
-    oqd_ref,
-    oql_ref,
-    ovd_ref,
-    ovl_ref,
+    out_ref,
     q_scr,
     g_scr,
     acts_scr,
@@ -80,7 +76,6 @@
     kt_scr,
     cost_scr,
     sint_scr,
-    dv_scr,
     dlq_scr,
     dlv_scr,
     ret_send,
@@ -254,28 +249,48 @@
         qr = q_scr[:, cols]
         g = g_scr[:, cols] * keep
         s = dot_nt(kwin[c], qr)
-        own = jnp.where(causal, s[:tok], NEG)
+        dp = dot_nt(vwin[c], g)
+        mid = tok // 2
+
+        def right_half(row, op, extra):
+            return jnp.concatenate([row[:, :mid], op(row[:, mid:], extra)], 1)
+
+        def key_max(x):
+            return jnp.max(x, 0, keepdims=True)
+
+        def key_sum(x):
+            return jnp.sum(x, 0, keepdims=True)
+
+        first = jnp.where(causal[:mid], s[:mid], NEG)
+        second = jnp.where(causal[:mid, :mid], s[mid:tok, mid:], NEG)
         prev = s[tok:]
-        top = jnp.maximum(
-            jnp.max(own, 0, keepdims=True), jnp.max(prev, 0, keepdims=True) + bias
-        )
+        top = jnp.maximum(key_max(first), key_max(prev) + bias)
+        top = right_half(top, jnp.maximum, key_max(second))
         shift = top * c2
-        e_own = jnp.exp2(own * c2 - shift)
-        e_prev = jnp.exp2(prev * c2 - (shift - bias))
-        total = jnp.sum(e_own, 0, keepdims=True) + jnp.sum(e_prev, 0, keepdims=True)
-        e = jnp.concatenate([e_own, e_prev], 0)
+        e1 = jnp.exp2(first * c2 - shift)
+        e2 = jnp.exp2(second * c2 - shift[:, mid:])
+        e3 = jnp.exp2(prev * c2 - (shift - bias))
+        total = right_half(key_sum(e1) + key_sum(e3), jnp.add, key_sum(e2))
         inverse = 1.0 / total
-        dp = dot_nt(vwin[c], g)
-        delta = jnp.sum(e * dp, 0, keepdims=True) * inverse
-        p = e * inverse
-        ds = (p * (dp - delta)).astype(BF16)
-        dv = dot(p.astype(BF16), g)
+        dp1, dp2, dp3 = dp[:mid], dp[mid:tok, mid:], dp[tok:]
+        delta = right_half(key_sum(e1 * dp1) + key_sum(e3 * dp3), jnp.add, key_sum(e2 * dp2))
+        delta = delta * inverse
+        p1, p2, p3 = e1 * inverse, e2 * inverse[:, mid:], e3 * inverse
+        none = jnp.zeros((tok - mid, mid), BF16)
+
+        def window(x1, x2, x3):
+            low = jnp.concatenate([none, x2.astype(BF16)], 1)
+            return jnp.concatenate([x1.astype(BF16), low, x3.astype(BF16)], 0)
+
+        p = window(p1, p2, p3)
+        ds = window(p1 * (dp1 - delta), p2 * (dp2 - delta[:, mid:]), p3 * (dp3 - delta))
         dq = dot(kt_scr[c], ds) * scaling
         half = HEAD // 2
         swapped = jnp.concatenate([dq[half:], dq[:half]], 0)
         dq_low = (dq * cost_scr[...] - swapped * sint_scr[...]).astype(BF16)
-        lift = ADAPTER_SCALE * dot_nt(qlt_ref[...], dq_low)
-        dlq = dot(qup_ref[:, cols], dq_low)
+        return p, g, dq_low
+
+    def write_lift(h, lift):
         if wq >= HEAD:
             slot = h * HEAD // wq
             at = pl.multiple_of(lax.rem(h * HEAD, wq), HEAD)
@@ -284,7 +299,6 @@
             per = HEAD // wq
             for j in range(per):
                 send_l[h * per + j, :, 0:HEAD] = lane_piece(lift, j, wq).astype(BF16)
-        return dv, dlq
 
     def to_seq(src, dst, ssem, rsem, peer):
         return pltpu.make_async_remote_copy(
@@ -301,28 +315,22 @@
             send_l.at[2 * z + 1 - side], got_l.at[z], l1_ssem.at[z], l1_rsem.at[z], partner
         )
 
-    unroll = 8
-
     def one_group(c, _):
-        dv_scr[...] = jnp.zeros_like(dv_scr)
         key_halo(c).wait()
         value_halo(c).wait()
         kt_scr[c, :, tok : 2 * tok] = kwin[c, tok : 2 * tok, :].astype(F32).T.astype(BF16)
 
-        def some_heads(step, _):
-            dvs = None
-            dlqs = None
-            for u in range(unroll):
-                dv, dlq = one_head(c, step * unroll + u)
-                dvs = dv if dvs is None else dvs + dv
-                dlqs = dlq if dlqs is None else dlqs + dlq
-            dv_scr[...] += dvs
-            dlq_scr[...] += dlqs
-            return 0
-
-        lax.fori_loop(0, heads // unroll, some_heads, 0)
+        parts = [one_head(c, i) for i in range(heads)]
+        probs = jnp.concatenate([part[0] for part in parts], 1)
+        grads = jnp.concatenate([part[1] for part in parts], 0)
+        turned = jnp.concatenate([part[2] for part in parts], 0)
+        dv_low = dot(probs, grads).astype(BF16)
+        span = heads * HEAD
+        dlq_scr[...] += dot(qup_ref[:, pl.ds(pl.multiple_of(c * span, span), span)], turned)
+        lifts = ADAPTER_SCALE * dot_nt(qlt_ref[...], turned)
+        for i in range(heads):
+            write_lift(c * heads + i, lifts[:, i * HEAD : (i + 1) * HEAD])
         kcols = pl.ds(pl.multiple_of(c * HEAD, HEAD), HEAD)
-        dv_low = dv_scr[...].astype(BF16)
         vup = vup_ref[:, kcols]
         dlv_scr[...] += dot_nt(vup, dv_low)
         vlift = ADAPTER_SCALE * (dot(vlt_ref[...], dv_low[:tok]) + dot(vlt_prev[...], dv_low[tok:]))
@@ -499,7 +507,6 @@
         return total + sq_recv[src]
 
     norm = jnp.sqrt(lax.fori_loop(1, n, gather_sq, sq_send[...]))
-    norm_ref[...] = norm
     factor = math.sqrt(PCOUNT) / (norm + STABLE)
     fac_send[...] = factor
     for k in range(1, m):
@@ -516,10 +523,14 @@
         other = fac_recv[src][0:1, 0:1]
         sum_d = sum_d + peer_d[src].astype(F32) * other
         sum_l = sum_l + peer_l[src].astype(F32) * other
-    oqd_ref[...] = sum_d[:half_rows] + NOISE_STD * nqd_ref[...]
-    ovd_ref[...] = sum_d[half_rows:] + NOISE_STD * nvd_ref[...]
-    oql_ref[...] = sum_l[:, 0:wq] + NOISE_STD * nql_ref[...]
-    ovl_ref[...] = sum_l[:, wqp : wqp + wv] + NOISE_STD * nvl_ref[...]
+    rank = half_rows
+    out_ref[0:rank, 0:wd] = sum_d[:rank] + NOISE_STD * nqd_ref[...]
+    out_ref[rank : 2 * rank, 0:wd] = sum_d[rank:] + NOISE_STD * nvd_ref[...]
+    out_ref[2 * rank : 3 * rank, 0:wq] = sum_l[:, 0:wq] + NOISE_STD * nql_ref[...]
+    out_ref[2 * rank : 3 * rank, wqp : wqp + wv] = (
+        sum_l[:, wqp : wqp + wv] + NOISE_STD * nvl_ref[...]
+    )
+    out_ref[3 * rank : 3 * rank + 8, 0:HEAD] = norm
 
     def finish_sq(k, _):
         sq_copy(lax.rem(me + k, n), me).wait_send()
@@ -548,6 +559,17 @@
         share_d_copy(peer, ex).wait_send()
         share_l_copy(peer, ex).wait_send()
         fac_copy(peer, ex).wait_send()
+
+
+def deliver(packed, out_norm, out_qd, out_ql, out_vd, out_vl):
+    rank, wd = out_qd.shape
+    wq = out_ql.shape[1]
+    at = max(wq, HEAD)
+    out_norm[0] = packed[3 * rank, 0]
+    out_qd[...] = packed[0:rank, 0:wd]
+    out_vd[...] = packed[rank : 2 * rank, 0:wd]
+    out_ql[...] = packed[2 * rank : 3 * rank, 0:wq]
+    out_vl[...] = packed[2 * rank : 3 * rank, at : at + out_vl.shape[1]]
 
 
 def body(
@@ -592,17 +614,11 @@
     smem = pl.BlockSpec(memory_space=pltpu.SMEM)
     hbm = pl.BlockSpec(memory_space=pltpu.HBM)
     dma = pltpu.SemaphoreType.DMA
-    norm, qd, ql, vd, vl = pl.pallas_call(
+    packed = pl.pallas_call(
         functools.partial(kernel, n, m),
-        out_shape=(
-            jax.ShapeDtypeStruct((8, HEAD), F32),
-            jax.ShapeDtypeStruct((rank, wd), F32),
-            jax.ShapeDtypeStruct((rank, wq), F32),
-            jax.ShapeDtypeStruct((rank, wd), F32),
-            jax.ShapeDtypeStruct((rank, wv), F32),
-        ),
+        out_shape=jax.ShapeDtypeStruct((3 * rank + 8, max(wd, wl)), F32),
         in_specs=[smem, smem] + [hbm] * 5 + [vmem] * 2 + [hbm] * 8,
-        out_specs=(vmem,) * 5,
+        out_specs=vmem,
         scratch_shapes=[
             pltpu.VMEM((tok, qw), BF16),
             pltpu.VMEM((tok, qw), BF16),
@@ -622,7 +638,6 @@
             pltpu.VMEM((groups, HEAD, 2 * tok), BF16),
             pltpu.VMEM((HEAD, tok), F32),
             pltpu.VMEM((HEAD, tok), F32),
-            pltpu.VMEM((2 * tok, HEAD), F32),
             pltpu.VMEM((rank, tok), F32),
             pltpu.VMEM((rank, 2 * tok), F32),
             pltpu.VMEM((rank, tok), F32),
@@ -677,7 +692,20 @@
         noise_value_down.T,
         noise_value_lift,
     )
-    return (norm[0, 0:1], qd.T, ql, vd.T, vl)
+    norm, qd, ql, vd, vl = pl.pallas_call(
+        deliver,
+        out_shape=(
+            jax.ShapeDtypeStruct((1,), F32),
+            jax.ShapeDtypeStruct((rank, wd), F32),
+            jax.ShapeDtypeStruct((rank, wq), F32),
+            jax.ShapeDtypeStruct((rank, wd), F32),
+            jax.ShapeDtypeStruct((rank, wv), F32),
+        ),
+        in_specs=[vmem],
+        out_specs=(smem,) + (vmem,) * 4,
+        name="deliver",
+    )(packed)
+    return (norm, qd.T, ql, vd.T, vl)
 
 
 def solution(mesh):

time: 67.4 us -> 57.7 us (0.86)
  local copies, waits for them, and re-layouts: 6.81 us -> 0 us
  Pallas kernels: 56.9 us -> 54.3 us
    unnamed x4 -> x0, local copies, waits for them, and re-layouts: 5.61 us -> none
    pallas_call x1 -> x2, Pallas kernels: 56.9 us -> 54.3 us  [the longest x1 52.7 us: body(): pl.pallas_call(functools.partial(kernel, n, m), out_shape=jax.ShapeDtypeS...]
    slice x1 -> x0, local copies, waits for them, and re-layouts: 1.19 us -> none  [body(): return (norm[0, 0:1], qd.T, ql, vd.T, vl)]
where the time goes in v3:
time: 57.7 us; the launch traced here: 57.5 us
  Pallas kernels  54.3 us (94%)
  between operations  1.95 us (3%)
  other arithmetic  1.33 us (2%)
    pallas_call x1, Pallas kernels, body(): pl.pallas_call(functools.partial(kernel, n, m), out_shape=jax.ShapeDtypeS...  52.7 us
    pallas_call x1, Pallas kernels, body(): pl.pallas_call(deliver, out_shape=(jax.ShapeDtypeStruct((1,), F32), jax.S...  1.61 us
    mul x1, other arithmetic, body(): sine = signs[None, :] * jnp.sin(angle)  1.24 us

profile of v3, /device:TPU:0, one launch (start us, length us, event | category | flops | bytes accessed | tf_op | source)
XLA Modules:
  0.0 57.5 jit_solution(11081323300975652045)
XLA Ops:
  1.9 0.1 compare_select_fusion
  2.0 1.2 %fusion = (f32[256,128]{1,0:T(8,128)}, f32[256,128]{1,0:T(8,128)}) fusion(f32[128]{0:T(128)S(1)} %get-tuple-element.17, f32[128]{0:T(128)S(1)} %get-tuple-element.18, f32[256]{0:T(256)S(1)} %add_convert_fusion), kind=kLoop, calls=%fused_computation.2 | loop fusion | flops 65536 | bytes 264192 | tf_op jit(solution)/shard_map/mul | solution.py:611
  3.3 52.7 %adapter_backward.1.packed = f32[56,1024]{1,0:T(8,128)} custom-call(s32[1,1]{1,0:T(1,128)S(6)} %copy.20.order_ref, s32[1]{0:T(128)S(6)} %copy.21.valid_ref, bf16[256,4096]{1,0:T(8,128)(2,1)} %bitcast.17, bf16[256,4096]{1,0:T(8,128)(2,1)} %bitcast.18, bf16[256,8192]{1,0:T(8,128)(2,1)} %bitcast.16, bf16[256,512]{1,0:T(8,128)(2,1)} %bitcast.19, ...), custom_call_target="tpu_custom_call" | custom-call | tf_op jit(solution)/shard_map/adapter_backward/pallas_call | solution.py:617
  55.9 1.6 %deliver.1 = (f32[1]{0:T(128)}, f32[16,1024]{1,0:T(8,128)}, f32[16,512]{1,0:T(8,128)}, f32[16,1024]{1,0:T(8,128)}, f32[16,64]{1,0:T(8,128)}) custom-call(f32[56,1024]{1,0:T(8,128)} %adapter_backward.1.packed), custom_call_target="tpu_custom_call" | custom-call | tf_op jit(solution)/shard_map/deliver/pallas_call | solution.py:695
  (2 shorter events, 0.0 us)
